TPU v7x, 32 devices: a whole 2x2x4 slice. The times are simulated.
32 devices in a mesh: lat: 4 (over y, x), lon: 2 (over core), ens: 4 (over z).
Axes of the slice: x: 2, y: 2, z: 4, core: 2. Of those that a mesh axis runs over, the one named last changes fastest.
Arguments:
- inputs: bfloat16 [4, 8, 1440, 256], P('ens', 'lat', 'lon'), may hold values from -12 to 12
- weight: bfloat16 [9, 256, 256], replicated, may hold values from -0.125 to 0.125
- spread: int32 [8], P('lat'), may hold values from 2 to 16, as said below
- target: bfloat16 [8, 1440, 256], P('lat', 'lon'), may hold values from -6 to 6
Outputs:
- response: bfloat16 [4, 8, 1440, 256], P('ens', 'lat', 'lon')
- grad_input: bfloat16 [4, 8, 1440, 256], P('ens', 'lat', 'lon')
- grad_weight: float32 [9, 256, 256], replicated
- loss: float32 [], replicated
Inputs may be any that keep to these rules, and one draw needn't show every extreme that they name: The filter of row o spans 2 spread[o] + 1 longitudes; spread is 16 on the 2 polar rows at each pole, which ignore it, and on the next row toward the equator.
All inputs are finite; a program needn't handle non-finite values.
Results may differ from a plain program's by a relative error of at most 0.009.
Values may be sent and summed in bfloat16 or wider, within the bound.
A program may use at most 128 MiB of HBM per device.

v0:
```python
import math

import jax
import jax.numpy as jnp
from jax import lax
from jax.sharding import PartitionSpec as P

PCAP = 2
HMAX = 16


highest = lax.Precision.HIGHEST


def extended_2(block, sides, width, periodic):
    for axis, dim in sides:
        count = lax.axis_size(axis)
        forward = [(i, i + 1) for i in range(count - 1)]
        if periodic:
            forward.append((count - 1, 0))
        backward = [(target, source) for source, target in forward]
        low = lax.ppermute(
            lax.slice_in_dim(block, block.shape[dim] - width, None, axis=dim), axis, forward
        )
        high = lax.ppermute(lax.slice_in_dim(block, 0, width, axis=dim), axis, backward)
        block = jnp.concatenate([low, block, high], axis=dim)
    return block


def kernel_rows(spread_rows, lon_count, reach):
    halves = spread_rows.astype(jnp.float32)[:, None, None, None] / 2.0
    columns = jnp.arange(lon_count)
    window_cols = jnp.arange(lon_count + 2 * reach)
    offsets = (window_cols[None, :] - reach - columns[:, None]).astype(jnp.float32)
    centres = (jnp.arange(3) - 1).astype(jnp.float32)[None, :, None, None] * halves
    values = jnp.maximum(0.0, 1.0 - jnp.abs(offsets[None, None] - centres) / halves) / halves
    return values.astype(jnp.bfloat16)


def circle_basis(first_col, lon_count, circle):
    angles = 2.0 * math.pi * (first_col + jnp.arange(lon_count)).astype(jnp.float32) / circle
    return jnp.stack([jnp.ones_like(angles), jnp.cos(angles), jnp.sin(angles)])


def circular(circle_sums, basis, circle, row_count):
    cos_wave = basis[1][None, None, :, None]
    sin_wave = basis[2][None, None, :, None]
    pieces = []
    for lat_tap in range(3):
        tap_sums = circle_sums[:, :, lat_tap : lat_tap + row_count]
        mean_part = tap_sums[:, 0][:, :, None, :] / circle
        cosine_part = (
            2.0
            / circle
            * (cos_wave * tap_sums[:, 1][:, :, None, :] + sin_wave * tap_sums[:, 2][:, :, None, :])
        )
        sine_part = (
            2.0
            / circle
            * (cos_wave * tap_sums[:, 2][:, :, None, :] - sin_wave * tap_sums[:, 1][:, :, None, :])
        )
        pieces += [jnp.broadcast_to(mean_part, cosine_part.shape), cosine_part, sine_part]
    return jnp.stack(pieces, 2)


def crps_terms(values, every_member, truth, lat_weight, member_total):
    miss = values - truth
    own_dist = jnp.sqrt(miss * miss + 0.25)
    own_slope = miss / own_dist

    def add_member(member, carry):
        pair_dist, pair_slope = carry
        other = lax.dynamic_index_in_dim(every_member, member, 0, keepdims=True).astype(jnp.float32)
        gap_value = values - other
        distance = jnp.sqrt(gap_value * gap_value + 0.25)
        return (pair_dist + distance, pair_slope + gap_value / distance)

    start = (jnp.zeros_like(values), jnp.zeros_like(values))
    pair_dist, pair_slope = lax.fori_loop(0, member_total, add_member, start)
    pair_dist = pair_dist - 0.5
    scores = own_dist / member_total - pair_dist / (2 * member_total * (member_total - 1))
    weighted = jnp.sum(lat_weight * scores)
    slopes = (
        lat_weight * (own_slope / member_total - pair_slope / (member_total * (member_total - 1)))
    ).astype(jnp.bfloat16)
    return (weighted, slopes)


def per_device(inputs, weight, spread, target):
    ens_local, row_count, lon_count, channels = inputs.shape
    reach = HMAX
    lat_total = row_count * lax.axis_size("lat")
    lon_total = lon_count * lax.axis_size("lon")
    lon_first = lax.axis_index("lon") * lon_count
    global_rows = lax.axis_index("lat") * row_count + jnp.arange(row_count)
    polar_rows = (global_rows < PCAP) | (global_rows >= lat_total - PCAP)
    polar_mask = polar_rows[None, :, None, None, None]
    kernels = kernel_rows(spread, lon_count, reach)
    local_basis = circle_basis(lon_first, lon_count, lon_total)
    extended = extended_2(inputs, (("lat", 1),), 1, False)
    window = extended_2(extended, (("lon", 2),), reach, True)
    local_sums = jnp.einsum(
        "pj,erjc->eprc", local_basis, extended.astype(jnp.float32), precision=highest
    )
    circle_sums = lax.psum(local_sums, "lon")
    banded = jnp.concatenate(
        [
            jnp.einsum(
                "objq,eoqc->eobjc",
                kernels,
                window[:, lat_tap : lat_tap + row_count],
                preferred_element_type=jnp.float32,
            )
            for lat_tap in range(3)
        ],
        2,
    )
    rounds = circular(circle_sums, local_basis, lon_total, row_count)
    features = jnp.where(polar_mask, rounds, banded).astype(jnp.bfloat16)
    response = jnp.einsum(
        "eokjc,kcd->eojd", features, weight, preferred_element_type=jnp.float32
    ).astype(jnp.bfloat16)
    member_total = ens_local * lax.axis_size("ens")
    row_weight = jnp.sin(math.pi * (global_rows.astype(jnp.float32) + 0.5) / lat_total)
    ensemble = lax.all_gather(response, "ens", axis=0, tiled=True)
    truth = target.astype(jnp.float32)[None]
    weighted, slopes = crps_terms(
        response.astype(jnp.float32), ensemble, truth, row_weight[None, :, None, None], member_total
    )
    loss_part = weighted / (lat_total * lon_total * channels)
    weight_part = jnp.einsum(
        "eokjc,eojd->kcd", features, slopes, preferred_element_type=jnp.float32
    )
    weight_sum, loss = lax.psum((weight_part, loss_part), ("lat", "lon", "ens"))
    grad_weight = weight_sum * math.sqrt(weight.shape[0] * channels) / (lat_total * lon_total)
    feature_grad = jnp.einsum(
        "eojd,kcd->eokjc", slopes, weight, preferred_element_type=jnp.float32
    ).astype(jnp.bfloat16)
    zero_grad = jnp.zeros_like(feature_grad)
    band_grad = jnp.where(polar_mask, zero_grad, feature_grad)
    circle_grad = jnp.where(polar_mask, feature_grad, zero_grad)
    window_grad = jnp.zeros(
        (ens_local, row_count + 2, lon_count + 2 * reach, channels), jnp.float32
    )
    sum_grad = jnp.zeros((ens_local, 3, row_count + 2, channels), jnp.float32)
    cos_wave = local_basis[1]
    sin_wave = local_basis[2]
    for lat_tap in range(3):
        picked = band_grad[:, :, 3 * lat_tap : 3 * lat_tap + 3]
        window_grad = window_grad.at[:, lat_tap : lat_tap + row_count].add(
            jnp.einsum("objq,eobjc->eoqc", kernels, picked, preferred_element_type=jnp.float32)
        )
        tap_grad = circle_grad[:, :, 3 * lat_tap : 3 * lat_tap + 3].astype(jnp.float32)
        mean_grad = jnp.sum(tap_grad[:, :, 0], axis=2) / lon_total
        cos_grad = (
            2.0
            / lon_total
            * (
                jnp.einsum("j,eojc->eoc", cos_wave, tap_grad[:, :, 1], precision=highest)
                - jnp.einsum("j,eojc->eoc", sin_wave, tap_grad[:, :, 2], precision=highest)
            )
        )
        sin_grad = (
            2.0
            / lon_total
            * (
                jnp.einsum("j,eojc->eoc", sin_wave, tap_grad[:, :, 1], precision=highest)
                + jnp.einsum("j,eojc->eoc", cos_wave, tap_grad[:, :, 2], precision=highest)
            )
        )
        sum_grad = sum_grad.at[:, :, lat_tap : lat_tap + row_count].add(
            jnp.stack([mean_grad, cos_grad, sin_grad], 1)
        )
    sum_total = lax.psum(sum_grad, "lon")
    core = window_grad[:, :, reach : reach + lon_count] + jnp.einsum(
        "pj,eprc->erjc", local_basis, sum_total, precision=highest
    )
    rims = jnp.concatenate([window_grad[:, :, :reach], window_grad[:, :, reach + lon_count :]], 2)
    arrived = extended_2(rims.astype(jnp.bfloat16), (("lon", 2),), reach, True).astype(rims.dtype)
    core = core.at[:, :, :reach].add(arrived[:, :, :reach])
    core = core.at[:, :, lon_count - reach :].add(arrived[:, :, 3 * reach :])
    edges = jnp.concatenate([core[:, :1], core[:, row_count + 1 :]], 1)
    arrived_rows = extended_2(edges.astype(jnp.bfloat16), (("lat", 1),), 1, False).astype(
        edges.dtype
    )
    inner = core[:, 1 : row_count + 1]
    inner = inner.at[:, 0].add(arrived_rows[:, 0])
    inner = inner.at[:, row_count - 1].add(arrived_rows[:, 3])
    return (response, inner.astype(jnp.bfloat16), grad_weight, loss)


def solution(mesh):
    in_specs = (P("ens", "lat", "lon", None), P(), P("lat"), P("lat", "lon", None))
    out_specs = (P("ens", "lat", "lon", None), P("ens", "lat", "lon", None), P(), P())
    return jax.shard_map(
        per_device, mesh=mesh, in_specs=in_specs, out_specs=out_specs, check_vma=False
    )
```

profile of v0, /device:TPU:0, one launch (start us, length us, event | category | flops | bytes accessed | tf_op | source)
XLA Modules:
  0.0 299.5 jit_solution(2205300542430974923)
XLA Ops:
  7.2 2.0 fusion.74
  9.2 5.6 %collective-permute-start = (bf16[1,1,720,256]{3,2,1,0:T(8,128)(2,1)S(1)}, bf16[1,1,720,256]{3,2,1,0:T(8,128)(2,1)}, u32[]{:S(2)}, u32[]{:S(2)}) collective-permute-start(bf16[1,1,720,256]{3,2,1,0:T(8,128)(2,1)S(1)} %get-tuple-element.265), channel_id=1, source_target_pairs={{0,8},{8,16},{16,24},{1,9},{9,17},{17,25},{2,10},{10,18},{18,26},{... | collective-permute-start | bytes 1105928 | tf_op jit(solution)/shard_map/ppermute | solution.py:22
  14.8 1.3 collective-permute-start.1
  16.2 0.7 convert_multiply_fusion.2
  16.8 1.6 subtract_convert_fusion
  18.6 3.3 %collective-permute-done = bf16[1,1,720,256]{3,2,1,0:T(8,128)(2,1)} collective-permute-done((bf16[1,1,720,256]{3,2,1,0:T(8,128)(2,1)S(1)}, bf16[1,1,720,256]{3,2,1,0:T(8,128)(2,1)}, u32[]{:S(2)}, u32[]{:S(2)}) %collective-permute-start) | collective-permute-done | bytes 368672 | tf_op jit(solution)/shard_map/ppermute | solution.py:22
  21.9 1.0 constant_dynamic-update-slice_fusion.2
  23.0 8.9 %collective-permute-done.1 = bf16[1,1,720,256]{3,2,1,0:T(8,128)(2,1)} collective-permute-done((bf16[1,1,720,256]{3,2,1,0:T(8,128)(2,1)}, bf16[1,1,720,256]{3,2,1,0:T(8,128)(2,1)}, u32[]{:S(2)}, u32[]{:S(2)}) %collective-permute-start.1) | collective-permute-done | bytes 368672 | tf_op jit(solution)/shard_map/ppermute | solution.py:25
  31.9 1.0 constant_dynamic-update-slice_fusion
  32.9 0.7 fusion.17
  33.6 3.4 %psum.28 = f32[1,3,4,256]{3,1,2,0:T(4,128)S(1)} all-reduce(f32[1,3,4,256]{3,1,2,0:T(4,128)S(1)} %fusion.17), channel_id=1, replica_groups=mesh['lat'=4,'lon'=2,'ens'=4] {'lon'}, use_global_device_ids=true, to_apply=%region_0.0 | all-reduce | flops 3072 | bytes 24576 | tf_op jit(solution)/shard_map/psum | solution.py:105
  37.1 0.3 multiply_dynamic-update-slice_fusion.5
  37.4 0.3 multiply_dynamic-update-slice_fusion.4
  38.4 0.4 collective-permute-start.2
  39.7 0.3 collective-permute-done.3
  40.1 0.8 copy-done.7
  41.0 3.2 %convolution_bitcast_fusion = bf16[2,3,720,256]{3,2,1,0:T(8,128)(2,1)S(1)} fusion(f32[2]{0:T(128)S(1)} %convert_multiply_fusion.2, f32[2,3]{1,0:T(2,128)S(1)} %broadcast_multiply_fusion.1, f32[720,752]{1,0:T(8,128)S(1)} %copy-done.7, bf16[1,4,752,256]{3,2,1,0:T(8,128)(2,1)S(1)} %pad_maximum_fusion), kind=kOutput, calls=%fused_computation.20 | convolution fusion | flops 1686044160 | bytes 5195264 | tf_op jit(solution)/shard_map/objq,eoqc->eobjc/dot_general | solution.py:108
  44.2 3.2 %convolution_bitcast_fusion.1 = bf16[2,3,720,256]{3,2,1,0:T(8,128)(2,1)S(1)} fusion(f32[2]{0:T(128)S(1)} %convert_multiply_fusion.2, f32[2,3]{1,0:T(2,128)S(1)} %broadcast_multiply_fusion.1, f32[720,752]{1,0:T(8,128)S(1)} %copy-done.7, bf16[1,4,752,256]{3,2,1,0:T(8,128)(2,1)S(1)} %pad_maximum_fusion), kind=kOutput, calls=%fused_computation.21 | convolution fusion | flops 1686044160 | bytes 5195264 | tf_op jit(solution)/shard_map/objq,eoqc->eobjc/dot_general | solution.py:108
  47.5 3.2 %convolution_bitcast_fusion.2 = bf16[2,3,720,256]{3,2,1,0:T(8,128)(2,1)S(1)} fusion(f32[2]{0:T(128)S(1)} %convert_multiply_fusion.2, f32[2,3]{1,0:T(2,128)S(1)} %broadcast_multiply_fusion.1, f32[720,752]{1,0:T(8,128)S(1)} %copy-done.7, bf16[1,4,752,256]{3,2,1,0:T(8,128)(2,1)S(1)} %pad_maximum_fusion), kind=kOutput, calls=%fused_computation.22 | convolution fusion | flops 1686044160 | bytes 5195264 | tf_op jit(solution)/shard_map/objq,eoqc->eobjc/dot_general | solution.py:108
  50.7 1.1 fusion
  51.9 2.7 copy-done.4
  54.6 2.8 bitcast_convert_fusion
  57.7 1.2 convert_bitcast_fusion
  59.0 59.2 %all-gather.3.cloned.1.call-done = bf16[8,720,256]{2,1,0:T(8,128)(2,1)} async-done(((bf16[2,720,256]{2,1,0:T(8,128)(2,1)}), bf16[8,720,256]{2,1,0:T(8,128)(2,1)}) %all-gather.3.cloned.1.call-update) | async-done | bytes 2949136 | tf_op jit(solution)/shard_map/all_gather | solution.py:125
  118.1 17.3 %while.26 = (s32[]{:T(128)}, f32[1,2,720,256]{3,2,1,0:T(8,128)}, f32[1,2,720,256]{3,2,1,0:T(8,128)}, bf16[4,2,720,256]{3,2,1,0:T(8,128)(2,1)}, f32[1,2,720,256]{3,2,1,0:T(8,128)S(1)}, /*index=5*/s32[]{:T(128)}, s32[]{:T(128)}) while((s32[]{:T(128)}, f32[1,2,720,256]{3,2,1,0:T(8,128)}, f32[1,2,720,256]{3,2,1,0:T(8,128)}, ...), condition=%wide.region_2.3_spmd.clone, body=%wide.region_1.2_spmd.clone.sunk | while | flops 3317763 | bytes 8110171 | solution.py:79
  118.1 3.7 %select_add_fusion.3 = (f32[1,2,720,256]{3,2,1,0:T(8,128)}, f32[1,2,720,256]{3,2,1,0:T(8,128)}) fusion(f32[1,2,720,256]{3,2,1,0:T(8,128)} %get-tuple-element.323, f32[1,2,720,256]{3,2,1,0:T(8,128)S(1)} %get-tuple-element.332, pred[]{:T(512)S(6)} %compare.63, bf16[4,2,720,256]{3,2,1,0:T(8,128)(2,1)} %get-tuple-element.331, s32[]{:T(128)} %get-tuple-element.321, ...), kind=kLoop, calls=%fused_computation.clone.1 | loop fusion | flops 3317760 | bytes 8110085 | tf_op jit(solution)/shard_map/while/body/eval_jaxpr/add | solution.py:76
  121.8 4.5 %select_add_fusion.3 = (f32[1,2,720,256]{3,2,1,0:T(8,128)}, f32[1,2,720,256]{3,2,1,0:T(8,128)}) fusion(f32[1,2,720,256]{3,2,1,0:T(8,128)} %get-tuple-element.323, f32[1,2,720,256]{3,2,1,0:T(8,128)S(1)} %get-tuple-element.332, pred[]{:T(512)S(6)} %compare.63, bf16[4,2,720,256]{3,2,1,0:T(8,128)(2,1)} %get-tuple-element.331, s32[]{:T(128)} %get-tuple-element.321, ...), kind=kLoop, calls=%fused_computation.clone.1 | loop fusion | flops 3317760 | bytes 8110085 | tf_op jit(solution)/shard_map/while/body/eval_jaxpr/add | solution.py:76
  126.3 4.5 %select_add_fusion.3 = (f32[1,2,720,256]{3,2,1,0:T(8,128)}, f32[1,2,720,256]{3,2,1,0:T(8,128)}) fusion(f32[1,2,720,256]{3,2,1,0:T(8,128)} %get-tuple-element.323, f32[1,2,720,256]{3,2,1,0:T(8,128)S(1)} %get-tuple-element.332, pred[]{:T(512)S(6)} %compare.63, bf16[4,2,720,256]{3,2,1,0:T(8,128)(2,1)} %get-tuple-element.331, s32[]{:T(128)} %get-tuple-element.321, ...), kind=kLoop, calls=%fused_computation.clone.1 | loop fusion | flops 3317760 | bytes 8110085 | tf_op jit(solution)/shard_map/while/body/eval_jaxpr/add | solution.py:76
  130.9 4.5 %select_add_fusion.3 = (f32[1,2,720,256]{3,2,1,0:T(8,128)}, f32[1,2,720,256]{3,2,1,0:T(8,128)}) fusion(f32[1,2,720,256]{3,2,1,0:T(8,128)} %get-tuple-element.323, f32[1,2,720,256]{3,2,1,0:T(8,128)S(1)} %get-tuple-element.332, pred[]{:T(512)S(6)} %compare.63, bf16[4,2,720,256]{3,2,1,0:T(8,128)(2,1)} %get-tuple-element.331, s32[]{:T(128)} %get-tuple-element.321, ...), kind=kLoop, calls=%fused_computation.clone.1 | loop fusion | flops 3317760 | bytes 8110085 | tf_op jit(solution)/shard_map/while/body/eval_jaxpr/add | solution.py:76
  135.4 3.9 %fusion.10 = (f32[]{:T(128)}, bf16[1,2,720,256]{3,2,1,0:T(8,128)(2,1)S(1)}) fusion(f32[1,2,720,256]{3,2,1,0:T(8,128)} %get-tuple-element.220, bf16[2,720,256]{2,1,0:T(8,128)(2,1)} %param.29, bf16[2,720,256]{2,1,0:T(8,128)(2,1)S(1)} %copy-done.5, f32[2]{0:T(128)S(1)} %multiply_sine_fusion, f32[1,2,720,256]{3,2,1,0:T(8,128)} %get-tuple-element.219), kind=kLoop, calls=%fused_computation.34 | loop fusion | flops 6266879 | bytes 5160972 | tf_op jit(solution)/shard_map/reduce_sum | solution.py:82
  139.3 6.4 %convolution_bitcast_fusion.3 = f32[9,256,256]{2,1,0:T(8,128)} fusion(bf16[2,9,720,256]{3,2,1,0:T(8,128)(2,1)} %copy-done.4, bf16[1,2,720,256]{3,2,1,0:T(8,128)(2,1)S(1)} %get-tuple-element.261), kind=kOutput, calls=%fused_computation.25 | convolution fusion | flops 1698693120 | bytes 9732096 | tf_op jit(solution)/shard_map/eokjc,eojd->kcd/dot_general | solution.py:131
  145.7 3.9 %fusion.2 = (bf16[1,2,9,720,256]{4,3,2,1,0:T(8,128)(2,1)S(1)}, bf16[1,2,9,720,256]{4,3,2,1,0:T(8,128)(2,1)}) fusion(pred[2]{0:T(512)(128)(4,1)S(1)} %compare_or_fusion, bf16[9,256,256]{2,1,0:T(8,128)(2,1)S(1)} %copy-done, bf16[1,2,720,256]{3,2,1,0:T(8,128)(2,1)S(1)} %get-tuple-element.261), kind=kOutput, calls=%fused_computation.10 | convolution fusion | flops 1708646400 | bytes 15187970 | tf_op jit(solution)/shard_map/eojd,kcd->eokjc/dot_general | solution.py:136
  149.6 0.4 fusion.35
  150.0 0.4 fusion.32
  150.4 0.4 fusion.33
  150.8 0.4 fusion.34
  151.2 0.4 fusion.29
  151.6 0.4 fusion.31
  152.0 0.4 fusion.28
  152.4 0.4 fusion.30
  152.8 0.4 fusion.25
  153.2 0.4 fusion.27
  153.6 0.4 fusion.24
  154.0 0.4 fusion.26
  154.4 0.3 convert_reduce_fusion
  154.7 1.3 copy-done.8
  156.0 5.7 %fusion.8 = f32[1,2,752,256]{3,2,1,0:T(8,128)S(1)} fusion(f32[2]{0:T(128)S(1)} %convert_multiply_fusion.2, f32[2,3]{1,0:T(2,128)S(1)} %broadcast_multiply_fusion.1, f32[720,752]{1,0:T(8,128)S(1)} %copy-done.8, bf16[1,2,9,720,256]{4,3,2,1,0:T(8,128)(2,1)} %get-tuple-element.255), kind=kOutput, calls=%fused_computation.31 | convolution fusion | flops 1686044160 | bytes 5917728 | tf_op jit(solution)/shard_map/objq,eobjc->eoqc/dot_general | solution.py:151
  161.9 5.9 %fusion.7 = f32[1,4,752,256]{3,2,1,0:T(8,128)S(1)} fusion(f32[1,4,752,256]{3,2,1,0:T(8,128)S(1)} %scatter-add.34, f32[2]{0:T(128)S(1)} %convert_multiply_fusion.2, f32[2,3]{1,0:T(2,128)S(1)} %broadcast_multiply_fusion.1, f32[720,752]{1,0:T(8,128)S(1)} %copy-done.8, bf16[1,2,9,720,256]{4,3,2,1,0:T(8,128)(2,1)} %get-tuple-element.255), kind=kOutput, calls=%fused_computation.30 | convolution fusion | flops 1686429184 | bytes 7505408 | tf_op jit(solution)/shard_map/objq,eobjc->eoqc/dot_general | solution.py:151
  167.9 5.7 %fusion.6 = f32[1,4,752,256]{3,2,1,0:T(8,128)S(1)} fusion(f32[1,4,752,256]{3,2,1,0:T(8,128)S(1)} %fusion.7, f32[2]{0:T(128)S(1)} %convert_multiply_fusion.2, f32[2,3]{1,0:T(2,128)S(1)} %broadcast_multiply_fusion.1, f32[720,752]{1,0:T(8,128)S(1)} %copy-done.8, bf16[1,2,9,720,256]{4,3,2,1,0:T(8,128)(2,1)} %get-tuple-element.255), kind=kOutput, calls=%fused_computation.27 | convolution fusion | flops 1686429184 | bytes 7505408 | tf_op jit(solution)/shard_map/objq,eobjc->eoqc/dot_general | solution.py:151
  173.5 1.6 copy-done.3
  175.6 3.4 %psum.29 = f32[3,4,256]{2,0,1:T(4,128)S(1)} all-reduce(f32[3,4,256]{2,0,1:T(4,128)S(1)} %fusion.39), channel_id=1, replica_groups=mesh['lat'=4,'lon'=2,'ens'=4] {'lon'}, use_global_device_ids=true, to_apply=%region_6.7 | all-reduce | flops 3072 | bytes 24576 | tf_op jit(solution)/shard_map/psum | solution.py:174
  178.9 4.5 %slice_add_fusion = f32[1,4,720,256]{3,2,1,0:T(8,128)S(1)} fusion(f32[1,4,752,256]{3,2,1,0:T(8,128)} %copy-done.3, f32[3,4,256]{2,0,1:T(4,128)S(1)} %psum.29, f32[1,720]{1,0:T(1,128)S(1)} %copy-done.10, f32[1,720]{1,0:T(1,128)S(1)} %copy-done.12, f32[3]{0:T(128)S(1)} %copy-done.14), kind=kOutput, calls=%fused_computation.12 | convolution fusion | flops 27283680 | bytes 5916300 | tf_op jit(solution)/shard_map/pj,eprc->erjc/dot_general | solution.py:175
  183.4 0.4 collective-permute-start.4
  184.0 0.7 collective-permute-done.4
  184.7 0.3 collective-permute-done.5
  185.1 1.6 copy-done.2
  186.7 3.4 %collective-permute-start.6 = (bf16[1,1,720,256]{3,2,1,0:T(8,128)(2,1)S(1)}, bf16[1,1,720,256]{3,2,1,0:T(8,128)(2,1)S(1)}, u32[]{:S(2)}, u32[]{:S(2)}) collective-permute-start(bf16[1,1,720,256]{3,2,1,0:T(8,128)(2,1)S(1)} %get-tuple-element.258), channel_id=1, source_target_pairs={{0,8},{8,16},{16,24},{1,9},{9,17},{17,25},{2,10},{10,18},{18,26},{... | collective-permute-start | bytes 1105928 | tf_op jit(solution)/shard_map/ppermute | solution.py:22
  190.1 1.3 collective-permute-start.7
  192.1 48.1 %psum.31 = f32[]{:T(128)} all-reduce(f32[]{:T(128)S(6)} %div.137), channel_id=1, replica_groups=mesh['lat'=4,'lon'=2,'ens'=4] {'lat','lon','ens'}, use_global_device_ids=true, to_apply=%region_9.10 | all-reduce | flops 1 | bytes 8 | tf_op jit(solution)/shard_map/psum | solution.py:134
  240.2 1.5 slice.533
  241.8 1.2 fusion.21
  243.1 0.9 convert_element_type.172
  244.0 45.3 %all-reduce.4.cloned.1.call-done = f32[9,256,256]{2,1,0:T(8,128)} async-done(((f32[9,256,256]{2,1,0:T(8,128)}), f32[9,256,256]{2,1,0:T(8,128)}) %all-reduce.4.cloned.1.call-update) | async-done | bytes 2359312 | tf_op jit(solution)/shard_map/psum | solution.py:134
  289.4 3.3 %broadcast_multiply_fusion = f32[9,256,256]{2,1,0:T(8,128)} fusion(f32[9,256,256]{2,1,0:T(8,128)} %all-reduce.4.cloned.1.call-done), kind=kLoop, calls=%fused_computation.53 | loop fusion | flops 589824 | bytes 4718592 | tf_op jit(solution)/shard_map/div | solution.py:135
  (93 shorter events, 3.3 us)
Async XLA Ops:
  7.2 47.4 %copy-start = (bf16[9,256,256]{2,1,0:T(8,128)(2,1)S(1)}, bf16[9,256,256]{2,1,0:T(8,128)(2,1)}, u32[]{:S(2)}) copy-start(bf16[9,256,256]{2,1,0:T(8,128)(2,1)} %param.27) | copy-start | bytes 3538948
  7.2 15.8 %copy-start.6 = (bf16[1,2,720,256]{3,2,1,0:T(8,128)(2,1)S(1)}, bf16[1,2,720,256]{3,2,1,0:T(8,128)(2,1)}, u32[]{:S(2)}) copy-start(bf16[1,2,720,256]{3,2,1,0:T(8,128)(2,1)} %param.26) | copy-start | bytes 2211844
  7.2 110.9 %all-gather.3.cloned.1.call-start = ((), (), s32[]{:S(2)}) async-start(), calls=%async_computation.1 | async-start | bytes 3686400 | tf_op jit(solution)/shard_map/all_gather | solution.py:125
  9.2 12.7 %collective-permute-start = (bf16[1,1,720,256]{3,2,1,0:T(8,128)(2,1)S(1)}, bf16[1,1,720,256]{3,2,1,0:T(8,128)(2,1)}, u32[]{:S(2)}, u32[]{:S(2)}) collective-permute-start(bf16[1,1,720,256]{3,2,1,0:T(8,128)(2,1)S(1)} %get-tuple-element.265), channel_id=1, source_target_pairs={{0,8},{8,16},{16,24},{1,9},{9,17},{17,25},{2,10},{10,18},{18,26},{... | collective-permute-start | bytes 1105928 | tf_op jit(solution)/shard_map/ppermute | solution.py:22
  14.8 17.0 %collective-permute-start.1 = (bf16[1,1,720,256]{3,2,1,0:T(8,128)(2,1)}, bf16[1,1,720,256]{3,2,1,0:T(8,128)(2,1)}, u32[]{:S(2)}, u32[]{:S(2)}) collective-permute-start(bf16[1,1,720,256]{3,2,1,0:T(8,128)(2,1)} %get-tuple-element.264), channel_id=1, source_target_pairs={{8,0},{16,8},{24,16},{9,1},{17,9},{25,17},{10,2},{18,10},{26,18},{... | collective-permute-start | bytes 1105928 | tf_op jit(solution)/shard_map/ppermute | solution.py:25
  18.5 14.3 %copy-start.9 = (f32[1,720]{1,0:T(1,128)}, f32[1,720]{1,0:T(1,128)S(1)}, u32[]{:S(2)}) copy-start(f32[1,720]{1,0:T(1,128)S(1)} %get-tuple-element.277) | copy-start | bytes 8644
  18.6 14.3 %copy-start.11 = (f32[1,720]{1,0:T(1,128)}, f32[1,720]{1,0:T(1,128)S(1)}, u32[]{:S(2)}) copy-start(f32[1,720]{1,0:T(1,128)S(1)} %get-tuple-element.278) | copy-start | bytes 8644
  18.6 14.3 %copy-start.13 = (f32[3]{0:T(128)}, f32[3]{0:T(128)S(1)}, u32[]{:S(2)}) copy-start(f32[3]{0:T(128)S(1)} %pad.47.clone) | copy-start | bytes 40
  38.4 1.3 collective-permute-start.2
  38.8 1.2 collective-permute-start.3
  39.3 1.6 copy-start.7
  51.8 2.7 copy-start.4
  57.4 232.0 %all-reduce.4.cloned.1.call-start = ((), (), s32[]{:S(2)}) async-start(), calls=%async_computation | async-start | bytes 4718592 | tf_op jit(solution)/shard_map/psum | solution.py:134
  118.1 17.3 %copy-start.5 = (bf16[2,720,256]{2,1,0:T(8,128)(2,1)S(1)}, bf16[2,720,256]{2,1,0:T(8,128)(2,1)}, u32[]{:S(2)}) copy-start(bf16[2,720,256]{2,1,0:T(8,128)(2,1)} %bitcast_convert_fusion) | copy-start | bytes 2211844
  154.4 1.6 copy-start.8
  167.8 11.1 %copy-start.10 = (f32[1,720]{1,0:T(1,128)S(1)}, f32[1,720]{1,0:T(1,128)}, u32[]{:S(2)}) copy-start(f32[1,720]{1,0:T(1,128)} %copy-done.9) | copy-start | bytes 8644
  167.8 11.1 %copy-start.12 = (f32[1,720]{1,0:T(1,128)S(1)}, f32[1,720]{1,0:T(1,128)}, u32[]{:S(2)}) copy-start(f32[1,720]{1,0:T(1,128)} %copy-done.11) | copy-start | bytes 8644
  167.8 11.1 %copy-start.14 = (f32[3]{0:T(128)S(1)}, f32[3]{0:T(128)}, u32[]{:S(2)}) copy-start(f32[3]{0:T(128)} %copy-done.13) | copy-start | bytes 40
  173.5 1.6 copy-start.3
  183.4 1.3 collective-permute-start.4
  183.8 1.2 collective-permute-start.5
  185.1 1.6 copy-start.2
  186.7 55.0 %collective-permute-start.6 = (bf16[1,1,720,256]{3,2,1,0:T(8,128)(2,1)S(1)}, bf16[1,1,720,256]{3,2,1,0:T(8,128)(2,1)S(1)}, u32[]{:S(2)}, u32[]{:S(2)}) collective-permute-start(bf16[1,1,720,256]{3,2,1,0:T(8,128)(2,1)S(1)} %get-tuple-element.258), channel_id=1, source_target_pairs={{0,8},{8,16},{16,24},{1,9},{9,17},{17,25},{2,10},{10,18},{18,26},{... | collective-permute-start | bytes 1105928 | tf_op jit(solution)/shard_map/ppermute | solution.py:22
  190.1 51.6 %collective-permute-start.7 = (bf16[1,1,720,256]{3,2,1,0:T(8,128)(2,1)S(1)}, bf16[1,1,720,256]{3,2,1,0:T(8,128)(2,1)S(1)}, u32[]{:S(2)}, u32[]{:S(2)}) collective-permute-start(bf16[1,1,720,256]{3,2,1,0:T(8,128)(2,1)S(1)} %get-tuple-element.259), channel_id=1, source_target_pairs={{8,0},{16,8},{24,16},{9,1},{17,9},{25,17},{10,2},{18,10},{26,18},{... | collective-permute-start | bytes 1105928 | tf_op jit(solution)/shard_map/ppermute | solution.py:25
  243.1 49.6 %copy-start.1 = (bf16[9,256,256]{2,1,0:T(8,128)(2,1)S(1)}, bf16[9,256,256]{2,1,0:T(8,128)(2,1)}, u32[]{:S(2)}) copy-start(bf16[9,256,256]{2,1,0:T(8,128)(2,1)} %param.27) | copy-start | bytes 3538948
Sparse Core Ops, SparseCore 0:
  57.5 60.5 all-gather.2
  154.9 134.4 all-reduce.3
where the time goes:
time: 300 us; the launch traced here: 299 us
  waiting for transfers between devices  118 us (39%)
  blocking collectives  54.8 us (18%)
  matrix products  50 us (17%)
  other arithmetic  33.9 us (11%)
  between operations  15.4 us (5%)
  local copies, waits for them, and re-layouts  14.3 us (5%)
  starting transfers between devices  13 us (4%)
    all_gather x1, waiting for transfers between devices, per_device(): ensemble = lax.all_gather(response, 'ens', axis=0, tiled=True)  59.2 us
    psum x1, blocking collectives, per_device(): weight_sum, loss = lax.psum((weight_part, loss_part), ('lat', 'lon', 'ens'))  48.1 us
    psum x1, waiting for transfers between devices, per_device(): weight_sum, loss = lax.psum((weight_part, loss_part), ('lat', 'lon', 'ens'))  45.3 us
    add x4, other arithmetic, add_member(): return (pair_dist + distance, pair_slope + gap_value / distance)  17.3 us
    dot_general x3, matrix products, per_device(): jnp.einsum('objq,eobjc->eoqc', kernels, picked, preferred_element_type=jn...  17.2 us
    ppermute x4, starting transfers between devices, extended_2(): lax.ppermute(lax.slice_in_dim(block, block.shape[dim] - width, None, axis...  9.8 us
    dot_general x3, matrix products, per_device(): jnp.einsum('objq,eoqc->eobjc', kernels, window[:, lat_tap:lat_tap + row_c...  9.71 us
    ppermute x4, waiting for transfers between devices, extended_2(): lax.ppermute(lax.slice_in_dim(block, 0, width, axis=dim), axis, backward)  9.56 us
  transfers between devices with their start and end apart: 10, of which 7 were waited for; matrix products, arithmetic and copies ran while one was open for 11% of the time, Pallas kernels for 0%

commit v1 on v0

--- a/solution.py
+++ b/solution.py
@@ -1,8 +1,11 @@
+import functools
 import math
 
 import jax
 import jax.numpy as jnp
 from jax import lax
+from jax.experimental import pallas as pl
+from jax.experimental.pallas import tpu as pltpu
 from jax.sharding import PartitionSpec as P
 
 PCAP = 2
@@ -84,6 +87,301 @@
         lat_weight * (own_slope / member_total - pair_slope / (member_total * (member_total - 1)))
     ).astype(jnp.bfloat16)
     return (weighted, slopes)
+
+
+MESH = pl.DeviceIdType.MESH
+ROWDOT = (((0,), (0,)), ((), ()))
+COLDOT = (((1,), (1,)), ((), ()))
+
+
+def pick_tile(lon_count):
+    for tile in (240, 144, 96, 80, 48, 32, 16):
+        if lon_count % tile == 0:
+            return tile
+    return 0
+
+
+def fits(row_count, lon_count, channels, taps):
+    lats, lons, members = (lax.axis_size(a) for a in ("lat", "lon", "ens"))
+    return (
+        lons == 2
+        and members <= 8
+        and lats <= 8
+        and channels % 256 == 0
+        and pick_tile(lon_count) > 0
+        and (taps * channels) % (16 * lats * members) == 0
+    )
+
+
+def middle(scale, feat, weight, target, row_weight, resp, fg, grad_w, loss, rsp, gath, acc, losses,
+           send1, recv1, out2, in2, red2, out3, in3, red3, full, sems, loss_sems):
+    members, lats = lax.axis_size("ens"), lax.axis_size("lat")
+    me, my_lat, my_lon = lax.axis_index("ens"), lax.axis_index("lat"), lax.axis_index("lon")
+    rows, taps, lon_count, channels = feat.shape
+    tile = pick_tile(lon_count)
+    per_row = lon_count // tile
+    chunks = rows * per_row
+    half = channels // 2
+
+    def peer(axis, here, count, step):
+        return {axis: lax.rem(here + step, count)}
+
+    barrier = pltpu.get_barrier_semaphore()
+    peers = (
+        [peer("ens", me, members, p) for p in range(1, members)]
+        + [peer("lat", my_lat, lats, p) for p in range(1, lats)]
+        + [{"lon": 1 - my_lon}]
+    )
+    for other in peers:
+        pl.semaphore_signal(barrier, inc=1, device_id=other, device_id_type=MESH)
+    pl.semaphore_wait(barrier, len(peers))
+
+    def where(i):
+        return i // per_row, pl.ds(pl.multiple_of(lax.rem(i, per_row) * tile, 16), tile)
+
+    def gather_copy(i, p):
+        o, cols = where(i)
+        return pltpu.make_async_remote_copy(
+            src_ref=rsp.at[o, cols], dst_ref=gath.at[p - 1, o, cols],
+            send_sem=send1.at[p - 1, i], recv_sem=recv1.at[p - 1, i],
+            device_id=peer("ens", me, members, p), device_id_type=MESH,
+        )
+
+    def forward(i, carry):
+        o, cols = where(i)
+        total = jnp.zeros((tile, channels), jnp.float32)
+        for k in range(taps):
+            total = total + jnp.dot(feat[o, k, cols], weight[k], preferred_element_type=jnp.float32)
+        rsp[o, cols] = total.astype(jnp.bfloat16)
+        for p in range(1, members):
+            gather_copy(i, p).start()
+        return carry
+
+    lax.fori_loop(0, chunks, forward, 0)
+    resp[...] = rsp[...]
+    acc[...] = jnp.zeros_like(acc)
+
+    def backward(i, carry):
+        o, cols = where(i)
+        for p in range(1, members):
+            gather_copy(i, p).wait_recv()
+        value = rsp[o, cols].astype(jnp.float32)
+        miss = value - target[o, cols].astype(jnp.float32)
+        square = miss * miss + 0.25
+        inverse = lax.rsqrt(square)
+        own_dist = square * inverse
+        own_slope = miss * inverse
+        pair_dist = jnp.zeros_like(value)
+        pair_slope = jnp.zeros_like(value)
+        for p in range(1, members):
+            gap = value - gath[p - 1, o, cols].astype(jnp.float32)
+            square = gap * gap + 0.25
+            inverse = lax.rsqrt(square)
+            pair_dist = pair_dist + square * inverse
+            pair_slope = pair_slope + gap * inverse
+        lat_weight = row_weight[o]
+        score = own_dist / members - pair_dist / (2 * members * (members - 1))
+        slope = lat_weight * (own_slope / members - pair_slope / (members * (members - 1)))
+        slope = slope.astype(jnp.bfloat16)
+        score = lat_weight * jnp.sum(score.reshape(tile // 8, 8, channels), axis=0)
+        for k in range(taps):
+            part = lax.dot_general(feat[o, k, cols], slope, ROWDOT, preferred_element_type=jnp.float32)
+            for h in range(2):
+                acc[h, pl.ds(k * channels, channels)] += part[:, h * half : (h + 1) * half]
+            fg[o, k, cols] = lax.dot_general(
+                slope, weight[k], COLDOT, preferred_element_type=jnp.float32
+            ).astype(jnp.bfloat16)
+        return carry + score
+
+    score = lax.fori_loop(0, chunks, backward, jnp.zeros((8, channels), jnp.float32))
+    part_loss = jnp.sum(score, axis=1, keepdims=True) * jnp.ones((8, 128), jnp.float32)
+
+    def remote(src, dst, at, other):
+        return pltpu.make_async_remote_copy(
+            src_ref=src, dst_ref=dst, send_sem=sems.at[0, at], recv_sem=sems.at[1, at],
+            device_id=other, device_id_type=MESH,
+        )
+
+    def remote_loss(src, dst, at, other):
+        return pltpu.make_async_remote_copy(
+            src_ref=src, dst_ref=dst, send_sem=loss_sems.at[0, at], recv_sem=loss_sems.at[1, at],
+            device_id=other, device_id_type=MESH,
+        )
+
+    def finish(copies):
+        for copy in copies:
+            copy.wait_recv()
+
+    pending = []
+    at, lat_at = 0, 0
+    out2[...] = acc[1 - my_lon].astype(jnp.bfloat16).reshape(out2.shape)
+    losses[0] = part_loss
+    copies = [
+        remote(out2, in2, at, {"lon": 1 - my_lon}),
+        remote_loss(losses.at[0], losses.at[1], lat_at, {"lon": 1 - my_lon}),
+    ]
+    for copy in copies:
+        copy.start()
+    finish(copies)
+    pending += copies
+    at, lat_at = at + 1, lat_at + 1
+    red2[...] = acc[my_lon].reshape(red2.shape) + in2[...].astype(jnp.float32)
+    base = 2
+    losses[base + my_lat] = losses[0] + losses[1]
+    send2 = out3
+    send2[...] = red2[...].astype(jnp.bfloat16)
+    copies = []
+    for p in range(1, lats):
+        other = peer("lat", my_lat, lats, p)
+        copies.append(remote(send2.at[other["lat"]], in3.at[p - 1], at, other))
+        copies.append(remote_loss(losses.at[base + my_lat], losses.at[base + my_lat], lat_at, other))
+        at, lat_at = at + 1, lat_at + 1
+    for copy in copies:
+        copy.start()
+    finish(copies)
+    pending += copies
+    total = red2[my_lat]
+    for p in range(1, lats):
+        total = total + in3[p - 1].astype(jnp.float32)
+    parts = red3.shape[0]
+    red3[...] = total.reshape(parts, total.shape[0] // parts, half)
+    total = losses[base]
+    for p in range(1, lats):
+        total = total + losses[base + p]
+    base = base + lats
+    losses[base + me] = total
+    red_out, red_in = full_split(full, members)
+    red_out[...] = red3[...].astype(jnp.bfloat16)
+    copies = []
+    for p in range(1, members):
+        other = peer("ens", me, members, p)
+        copies.append(remote(red_out.at[other["ens"]], red_in.at[p - 1], at, other))
+        copies.append(remote_loss(losses.at[base + me], losses.at[base + me], lat_at, other))
+        at, lat_at = at + 1, lat_at + 1
+    for copy in copies:
+        copy.start()
+    finish(copies)
+    pending += copies
+    total = red3[me]
+    for p in range(1, members):
+        total = total + red_in[p - 1].astype(jnp.float32)
+    gathered = full[2]
+    gathered[my_lon, my_lat, me] = (total * scale).astype(jnp.bfloat16)
+    total = losses[base]
+    for p in range(1, members):
+        total = total + losses[base + p]
+    loss[...] = total
+    mine = gathered.at[my_lon, my_lat, me]
+    copies = []
+    for p in range(1, members):
+        copies.append(remote(mine, mine, at, peer("ens", me, members, p)))
+        at += 1
+    for copy in copies:
+        copy.start()
+    finish(copies)
+    pending += copies
+    mine = gathered.at[my_lon, my_lat]
+    copies = []
+    for p in range(1, lats):
+        copies.append(remote(mine, mine, at, peer("lat", my_lat, lats, p)))
+        at += 1
+    for copy in copies:
+        copy.start()
+    finish(copies)
+    pending += copies
+    mine = gathered.at[my_lon]
+    copies = [remote(mine, mine, at, {"lon": 1 - my_lon})]
+    copies[0].start()
+    finish(copies)
+    pending += copies
+    for h in range(2):
+        grad_w[:, :, h * half : (h + 1) * half] = (
+            gathered[h].astype(jnp.float32).reshape(taps, channels, half)
+        )
+    for copy in pending:
+        copy.wait_send()
+
+    def drain(i, carry):
+        for p in range(1, members):
+            gather_copy(i, p).wait_send()
+        return carry
+
+    lax.fori_loop(0, chunks, drain, 0)
+
+
+def full_split(full, members):
+    return full[0], full[1]
+
+
+def run_middle(scale, feat, weight, target, row_weight):
+    members, lats = lax.axis_size("ens"), lax.axis_size("lat")
+    rows, taps, lon_count, channels = feat.shape
+    chunks = rows * (lon_count // pick_tile(lon_count))
+    half = channels // 2
+    flat = taps * channels
+    band, piece = flat // lats, flat // lats // members
+    bf16, f32 = jnp.bfloat16, jnp.float32
+    shape = jax.ShapeDtypeStruct
+    whole = pl.BlockSpec(memory_space=pltpu.VMEM)
+    count = 1 + 2 * (lats - 1) + 2 * (members - 1) + 1
+    loss_count = 1 + (lats - 1) + (members - 1)
+    return pl.pallas_call(
+        functools.partial(middle, scale),
+        out_shape=[
+            shape((rows, lon_count, channels), bf16),
+            shape(feat.shape, bf16),
+            shape((taps, channels, channels), f32),
+            shape((8, 128), f32),
+        ],
+        in_specs=[whole] * 4,
+        out_specs=[whole] * 4,
+        scratch_shapes=[
+            pltpu.VMEM((rows, lon_count, channels), bf16),
+            pltpu.VMEM((members - 1, rows, lon_count, channels), bf16),
+            pltpu.VMEM((2, flat, half), f32),
+            pltpu.VMEM((2 + lats + members, 8, 128), f32),
+            pltpu.SemaphoreType.DMA((members - 1, chunks)),
+            pltpu.SemaphoreType.DMA((members - 1, chunks)),
+            pltpu.VMEM((lats, band, half), bf16),
+            pltpu.VMEM((lats, band, half), bf16),
+            pltpu.VMEM((lats, band, half), f32),
+            pltpu.VMEM((lats, band, half), bf16),
+            pltpu.VMEM((lats - 1, band, half), bf16),
+            pltpu.VMEM((members, piece, half), f32),
+            [
+                pltpu.VMEM((members, piece, half), bf16),
+                pltpu.VMEM((members - 1, piece, half), bf16),
+                pltpu.VMEM((2, lats, members, piece, half), bf16),
+            ],
+            pltpu.SemaphoreType.DMA((2, count)),
+            pltpu.SemaphoreType.DMA((2, loss_count)),
+        ],
+        compiler_params=pltpu.CompilerParams(
+            collective_id=0, has_side_effects=True, vmem_limit_bytes=50 * 1024 * 1024
+        ),
+        name="middle",
+    )(feat, weight, target, row_weight)
+
+
+def plain_middle(features, weight, target, row_weight, scale, cells):
+    response = jnp.einsum(
+        "eokjc,kcd->eojd", features, weight, preferred_element_type=jnp.float32
+    ).astype(jnp.bfloat16)
+    member_total = features.shape[0] * lax.axis_size("ens")
+    ensemble = lax.all_gather(response, "ens", axis=0, tiled=True)
+    truth = target.astype(jnp.float32)[None]
+    weighted, slopes = crps_terms(
+        response.astype(jnp.float32), ensemble, truth, row_weight[None, :, None, None], member_total
+    )
+    loss_part = weighted / cells
+    weight_part = jnp.einsum(
+        "eokjc,eojd->kcd", features, slopes, preferred_element_type=jnp.float32
+    )
+    weight_sum, loss = lax.psum((weight_part, loss_part), ("lat", "lon", "ens"))
+    feature_grad = jnp.einsum(
+        "eojd,kcd->eokjc", slopes, weight, preferred_element_type=jnp.float32
+    ).astype(jnp.bfloat16)
+    return response, feature_grad, weight_sum * scale, loss
 
 
 def per_device(inputs, weight, spread, target):
@@ -117,25 +415,19 @@
     )
     rounds = circular(circle_sums, local_basis, lon_total, row_count)
     features = jnp.where(polar_mask, rounds, banded).astype(jnp.bfloat16)
-    response = jnp.einsum(
-        "eokjc,kcd->eojd", features, weight, preferred_element_type=jnp.float32
-    ).astype(jnp.bfloat16)
-    member_total = ens_local * lax.axis_size("ens")
-    row_weight = jnp.sin(math.pi * (global_rows.astype(jnp.float32) + 0.5) / lat_total)
-    ensemble = lax.all_gather(response, "ens", axis=0, tiled=True)
-    truth = target.astype(jnp.float32)[None]
-    weighted, slopes = crps_terms(
-        response.astype(jnp.float32), ensemble, truth, row_weight[None, :, None, None], member_total
-    )
-    loss_part = weighted / (lat_total * lon_total * channels)
-    weight_part = jnp.einsum(
-        "eokjc,eojd->kcd", features, slopes, preferred_element_type=jnp.float32
-    )
-    weight_sum, loss = lax.psum((weight_part, loss_part), ("lat", "lon", "ens"))
-    grad_weight = weight_sum * math.sqrt(weight.shape[0] * channels) / (lat_total * lon_total)
-    feature_grad = jnp.einsum(
-        "eojd,kcd->eokjc", slopes, weight, preferred_element_type=jnp.float32
-    ).astype(jnp.bfloat16)
+    lat_weight = jnp.sin(math.pi * (global_rows.astype(jnp.float32) + 0.5) / lat_total)
+    scale = math.sqrt(weight.shape[0] * channels) / (lat_total * lon_total)
+    if ens_local == 1 and fits(row_count, lon_count, channels, weight.shape[0]):
+        wide = jnp.broadcast_to(lat_weight[:, None, None], (row_count, 1, channels))
+        response, feature_grad, grad_weight, loss_parts = run_middle(
+            scale, features[0], weight, target, wide
+        )
+        response, feature_grad = response[None], feature_grad[None]
+        loss = jnp.sum(loss_parts[:, 0]) / (lat_total * lon_total * channels)
+    else:
+        response, feature_grad, grad_weight, loss = plain_middle(
+            features, weight, target, lat_weight, scale, lat_total * lon_total * channels
+        )
     zero_grad = jnp.zeros_like(feature_grad)
     band_grad = jnp.where(polar_mask, zero_grad, feature_grad)
     circle_grad = jnp.where(polar_mask, feature_grad, zero_grad)

time: 300 us -> 231 us (0.77)
  Pallas kernels: 0 us -> 113 us
  waiting for transfers between devices: 118 us -> 19.5 us
  blocking collectives: 54.8 us -> 7.13 us
  other arithmetic: 33.9 us -> 19.9 us
  between operations: 15.4 us -> 3.12 us
  local copies, waits for them, and re-layouts: 14.3 us -> 8.35 us
  matrix products: 50 us -> 45.9 us
    pallas_call x0 -> x1, Pallas kernels: none -> 113 us  [run_middle(): pl.pallas_call(functools.partial(middle, scale), out_shape=[shape((rows,...]
    all_gather x1 -> x0, waiting for transfers between devices: 59.2 us -> none  [per_device(): ensemble = lax.all_gather(response, 'ens', axis=0, tiled=True)]
    psum x1 -> x0, blocking collectives: 48.1 us -> none  [per_device(): weight_sum, loss = lax.psum((weight_part, loss_part), ('lat', 'lon', 'ens'))]
    psum x1 -> x0, waiting for transfers between devices: 45.3 us -> none  [per_device(): weight_sum, loss = lax.psum((weight_part, loss_part), ('lat', 'lon', 'ens'))]
    add x4 -> x0, other arithmetic: 17.3 us -> none  [add_member(): return (pair_dist + distance, pair_slope + gap_value / distance)]
    dot_general x3 -> x0, matrix products: 13.1 us -> none  [the longest x1 6.37 us: per_device(): jnp.einsum('eokjc,eojd->kcd', features, slopes, preferred_element_type=jn...]
    select_n x0 -> x1, other arithmetic: none -> 8.55 us  [per_device(): circle_grad = jnp.where(polar_mask, feature_grad, zero_grad)]
    ppermute x4, waiting for transfers between devices: 4.01 us -> 10.1 us  [extended_2(): lax.ppermute(lax.slice_in_dim(block, block.shape[dim] - width, None, axis...]
  transfers between devices with their start and end apart: 10 -> 8, of which waited for: 7 -> 5; matrix products, arithmetic and copies ran while one was open for 11% -> 3% of each run, Pallas kernels for 0% -> 0%
where the time goes in v1:
time: 231 us; the launch traced here: 230 us
  Pallas kernels  113 us (49%)
  matrix products  45.9 us (20%)
  other arithmetic  19.9 us (9%)
  waiting for transfers between devices  19.5 us (8%)
  starting transfers between devices  12.6 us (5%)
  local copies, waits for them, and re-layouts  8.35 us (4%)
  blocking collectives  7.13 us (3%)
  between operations  3.12 us (1%)
    pallas_call x1, Pallas kernels, run_middle(): pl.pallas_call(functools.partial(middle, scale), out_shape=[shape((rows,...  113 us
    dot_general x3, matrix products, per_device(): jnp.einsum('objq,eobjc->eoqc', kernels, picked, preferred_element_type=jn...  17.4 us
    ppermute x4, waiting for transfers between devices, extended_2(): lax.ppermute(lax.slice_in_dim(block, block.shape[dim] - width, None, axis...  10.1 us
    dot_general x3, matrix products, per_device(): jnp.einsum('objq,eoqc->eobjc', kernels, window[:, lat_tap:lat_tap + row_c...  9.71 us
    ppermute x4, starting transfers between devices, extended_2(): lax.ppermute(lax.slice_in_dim(block, block.shape[dim] - width, None, axis...  9.52 us
    ppermute x4, waiting for transfers between devices, extended_2(): lax.ppermute(lax.slice_in_dim(block, 0, width, axis=dim), axis, backward)  9.39 us
    select_n x1, other arithmetic, per_device(): circle_grad = jnp.where(polar_mask, feature_grad, zero_grad)  8.55 us
    unnamed x44, local copies, waits for them, and re-layouts  5.07 us
  transfers between devices with their start and end apart: 8, of which 5 were waited for; matrix products, arithmetic and copies ran while one was open for 3% of the time, Pallas kernels for 0%

profile of v1, /device:TPU:0, one launch (start us, length us, event | category | flops | bytes accessed | tf_op | source)
XLA Modules:
  0.0 229.8 jit_solution(15942239960276304424)
XLA Ops:
  0.6 1.2 fusion.64
  1.9 1.3 collective-permute-start.1
  3.2 5.5 %collective-permute-start = (bf16[1,1,720,256]{3,2,1,0:T(8,128)(2,1)S(1)}, bf16[1,1,720,256]{3,2,1,0:T(8,128)(2,1)S(1)}, u32[]{:S(2)}, u32[]{:S(2)}) collective-permute-start(bf16[1,1,720,256]{3,2,1,0:T(8,128)(2,1)S(1)} %get-tuple-element.144), channel_id=1, source_target_pairs={{0,8},{8,16},{16,24},{1,9},{9,17},{17,25},{2,10},{10,18},{18,26},{... | collective-permute-start | bytes 1105928 | tf_op jit(solution)/shard_map/ppermute | solution.py:25
  8.7 0.7 convert_multiply_fusion.2
  9.4 1.6 subtract_convert_fusion
  10.9 0.1 broadcast_multiply_fusion
  11.1 0.1 fusion.45
  11.3 5.2 %collective-permute-done = bf16[1,1,720,256]{3,2,1,0:T(8,128)(2,1)S(1)} collective-permute-done((bf16[1,1,720,256]{3,2,1,0:T(8,128)(2,1)S(1)}, bf16[1,1,720,256]{3,2,1,0:T(8,128)(2,1)S(1)}, u32[]{:S(2)}, u32[]{:S(2)}) %collective-permute-start) | collective-permute-done | bytes 368672 | tf_op jit(solution)/shard_map/ppermute | solution.py:25
  16.6 0.7 fusion.9
  17.4 3.4 %psum.14 = f32[1,3,4,256]{3,1,2,0:T(4,128)S(1)} all-reduce(f32[1,3,4,256]{3,1,2,0:T(4,128)S(1)} %fusion.9), channel_id=1, replica_groups=mesh['lat'=4,'lon'=2,'ens'=4] {'lon'}, use_global_device_ids=true, to_apply=%region_0.0 | all-reduce | flops 3072 | bytes 24576 | tf_op jit(solution)/shard_map/psum | solution.py:403
  20.9 0.4 collective-permute-start.2
  21.3 0.2 collective-permute-start.3
  21.5 0.3 multiply_dynamic-update-slice_fusion.5
  21.8 0.3 multiply_dynamic-update-slice_fusion.4
  22.1 0.3 multiply_dynamic-update-slice_fusion.3
  22.4 0.3 multiply_dynamic-update-slice_fusion.2
  22.8 0.3 multiply_dynamic-update-slice_fusion.1
  23.1 0.3 multiply_dynamic-update-slice_fusion
  23.4 0.1 pad_maximum_fusion
  23.5 0.9 copy-done.6
  24.4 3.2 %convolution_bitcast_fusion.1 = bf16[2,3,720,256]{3,2,1,0:T(8,128)(2,1)S(1)} fusion(f32[2]{0:T(128)S(1)} %convert_multiply_fusion.2, f32[2,3]{1,0:T(2,128)S(1)} %broadcast_multiply_fusion, f32[720,752]{1,0:T(8,128)S(1)} %copy-done.6, bf16[1,4,752,256]{3,2,1,0:T(8,128)(2,1)S(1)} %pad_maximum_fusion), kind=kOutput, calls=%fused_computation.14 | convolution fusion | flops 1686044160 | bytes 5195264 | tf_op jit(solution)/shard_map/objq,eoqc->eobjc/dot_general | solution.py:406
  27.6 3.2 %convolution_bitcast_fusion = bf16[2,3,720,256]{3,2,1,0:T(8,128)(2,1)S(1)} fusion(f32[2]{0:T(128)S(1)} %convert_multiply_fusion.2, f32[2,3]{1,0:T(2,128)S(1)} %broadcast_multiply_fusion, f32[720,752]{1,0:T(8,128)S(1)} %copy-done.6, bf16[1,4,752,256]{3,2,1,0:T(8,128)(2,1)S(1)} %pad_maximum_fusion), kind=kOutput, calls=%fused_computation.13 | convolution fusion | flops 1686044160 | bytes 5195264 | tf_op jit(solution)/shard_map/objq,eoqc->eobjc/dot_general | solution.py:406
  30.9 3.2 %convolution_bitcast_fusion.2 = bf16[2,3,720,256]{3,2,1,0:T(8,128)(2,1)S(1)} fusion(f32[2]{0:T(128)S(1)} %convert_multiply_fusion.2, f32[2,3]{1,0:T(2,128)S(1)} %broadcast_multiply_fusion, f32[720,752]{1,0:T(8,128)S(1)} %copy-done.6, bf16[1,4,752,256]{3,2,1,0:T(8,128)(2,1)S(1)} %pad_maximum_fusion), kind=kOutput, calls=%fused_computation.15 | convolution fusion | flops 1686044160 | bytes 5195264 | tf_op jit(solution)/shard_map/objq,eoqc->eobjc/dot_general | solution.py:406
  34.2 3.6 %fusion.feat = bf16[2,9,720,256]{3,2,1,0:T(8,128)(2,1)} fusion(bf16[2,9,720,256]{3,2,1,0:T(8,128)(2,1)S(1)} %multiply_dynamic-update-slice_fusion, bf16[2,3,720,256]{3,2,1,0:T(8,128)(2,1)S(1)} %convolution_bitcast_fusion, bf16[2,3,720,256]{3,2,1,0:T(8,128)(2,1)S(1)} %convolution_bitcast_fusion.1, bf16[2,3,720,256]{3,2,1,0:T(8,128)(2,1)S(1)} %convolution_bitcast_fusion.2, ...), kind=kLoop, calls=%fused_computation.1 | loop fusion | flops 9953280 | bytes 19906562 | tf_op jit(solution)/shard_map/convert_element_type | solution.py:417
  37.8 113.4 %middle.1 = (bf16[2,720,256]{2,1,0:T(8,128)(2,1)S(1)}, bf16[2,9,720,256]{3,2,1,0:T(8,128)(2,1)}, f32[9,256,256]{2,1,0:T(8,128)}, f32[8,128]{1,0:T(8,128)S(1)}) custom-call(bf16[2,9,720,256]{3,2,1,0:T(8,128)(2,1)} %fusion.feat, bf16[9,256,256]{2,1,0:T(8,128)(2,1)S(1)} %copy-done, bf16[2,720,256]{2,1,0:T(8,128)(2,1)S(1)} %copy-done.1, ...), custom_call_target="tpu_custom_call" | custom-call | tf_op jit(solution)/shard_map/middle/pallas_call | solution.py:328
  151.3 8.6 %select_bitcast_fusion = (bf16[1,2,9,720,256]{4,3,2,1,0:T(8,128)(2,1)}, bf16[1,2,9,720,256]{4,3,2,1,0:T(8,128)(2,1)}) fusion(bf16[2,9,720,256]{3,2,1,0:T(8,128)(2,1)} %get-tuple-element.129, pred[2]{0:T(512)(128)(4,1)S(1)} %compare_or_fusion), kind=kLoop, calls=%fused_computation.3 | loop fusion | flops 6635520 | bytes 19906562 | tf_op jit(solution)/shard_map/jit(_where)/select_n | solution.py:433
  159.8 1.6 fusion.20
  161.5 1.9 fusion.16
  163.4 1.5 fusion.18
  164.9 1.5 fusion.14
  166.4 1.5 fusion.25
  167.9 1.5 fusion.23
  169.4 1.5 fusion.21
  170.9 1.7 fusion.19
  172.6 1.5 fusion.24
  174.1 0.4 fusion.15
  174.5 0.4 fusion.17
  174.9 0.4 fusion.22
  175.3 0.3 convert_reduce_fusion
  175.8 0.2 scatter-add.40
  176.0 3.8 %psum.15 = f32[3,4,256]{2,0,1:T(4,128)S(1)} all-reduce(f32[3,4,256]{2,0,1:T(4,128)S(1)} %fusion.29), channel_id=1, replica_groups=mesh['lat'=4,'lon'=2,'ens'=4] {'lon'}, use_global_device_ids=true, to_apply=%region_4.5 | all-reduce | flops 3072 | bytes 24576 | tf_op jit(solution)/shard_map/psum | solution.py:466
  179.8 6.0 %fusion.6 = f32[1,2,752,256]{3,2,1,0:T(8,128)S(1)} fusion(f32[2]{0:T(128)S(1)} %convert_multiply_fusion.2, f32[2,3]{1,0:T(2,128)S(1)} %broadcast_multiply_fusion, f32[720,752]{1,0:T(8,128)S(1)} %copy-done.7, bf16[1,2,9,720,256]{4,3,2,1,0:T(8,128)(2,1)} %get-tuple-element.136), kind=kOutput, calls=%fused_computation.21 | convolution fusion | flops 1686044160 | bytes 5917728 | tf_op jit(solution)/shard_map/objq,eobjc->eoqc/dot_general | solution.py:443
  185.8 0.2 scatter-add.34
  186.0 5.7 %fusion.5 = f32[1,4,752,256]{3,2,1,0:T(8,128)S(1)} fusion(f32[1,4,752,256]{3,2,1,0:T(8,128)S(1)} %scatter-add.34, f32[2]{0:T(128)S(1)} %convert_multiply_fusion.2, f32[2,3]{1,0:T(2,128)S(1)} %broadcast_multiply_fusion, f32[720,752]{1,0:T(8,128)S(1)} %copy-done.7, bf16[1,2,9,720,256]{4,3,2,1,0:T(8,128)(2,1)} %get-tuple-element.136), kind=kOutput, calls=%fused_computation.20 | convolution fusion | flops 1686429184 | bytes 7505408 | tf_op jit(solution)/shard_map/objq,eobjc->eoqc/dot_general | solution.py:443
  191.7 5.7 %fusion.4 = f32[1,4,752,256]{3,2,1,0:T(8,128)S(1)} fusion(f32[1,4,752,256]{3,2,1,0:T(8,128)S(1)} %fusion.5, f32[2]{0:T(128)S(1)} %convert_multiply_fusion.2, f32[2,3]{1,0:T(2,128)S(1)} %broadcast_multiply_fusion, f32[720,752]{1,0:T(8,128)S(1)} %copy-done.7, bf16[1,2,9,720,256]{4,3,2,1,0:T(8,128)(2,1)} %get-tuple-element.136), kind=kOutput, calls=%fused_computation.17 | convolution fusion | flops 1686429184 | bytes 7505408 | tf_op jit(solution)/shard_map/objq,eobjc->eoqc/dot_general | solution.py:443
  197.5 2.6 %slice_add_fusion = f32[1,4,720,256]{3,2,1,0:T(8,128)S(1)} fusion(f32[1,4,752,256]{3,2,1,0:T(8,128)S(1)} %fusion.4, f32[3,4,256]{2,0,1:T(4,128)S(1)} %psum.15, f32[1,720]{1,0:T(1,128)S(1)} %copy-done.9, f32[1,720]{1,0:T(1,128)S(1)} %copy-done.11, f32[3]{0:T(128)S(1)} %copy-done.13), kind=kOutput, calls=%fused_computation.5 | convolution fusion | flops 27283680 | bytes 5916300 | tf_op jit(solution)/shard_map/pj,eprc->erjc/dot_general | solution.py:467
  200.1 0.2 collective-permute-start.4
  200.3 0.3 collective-permute-start.5
  200.7 0.7 collective-permute-done.4
  201.4 0.2 collective-permute-done.5
  201.6 1.6 copy-done.3
  203.2 0.1 fusion.62
  203.2 3.4 %collective-permute-start.6 = (bf16[1,1,720,256]{3,2,1,0:T(8,128)(2,1)S(1)}, bf16[1,1,720,256]{3,2,1,0:T(8,128)(2,1)S(1)}, u32[]{:S(2)}, u32[]{:S(2)}) collective-permute-start(bf16[1,1,720,256]{3,2,1,0:T(8,128)(2,1)S(1)} %get-tuple-element.139), channel_id=1, source_target_pairs={{0,8},{8,16},{16,24},{1,9},{9,17},{17,25},{2,10},{10,18},{18,26},{... | collective-permute-start | bytes 1105928 | tf_op jit(solution)/shard_map/ppermute | solution.py:25
  206.6 1.3 collective-permute-start.7
  207.9 0.6 slice_reduce_fusion
  209.2 1.5 slice.537
  210.7 0.1 maximum_bitcast_fusion
  210.7 4.2 %collective-permute-done.6 = bf16[1,1,720,256]{3,2,1,0:T(8,128)(2,1)S(1)} collective-permute-done((bf16[1,1,720,256]{3,2,1,0:T(8,128)(2,1)S(1)}, bf16[1,1,720,256]{3,2,1,0:T(8,128)(2,1)S(1)}, u32[]{:S(2)}, u32[]{:S(2)}) %collective-permute-start.6) | collective-permute-done | bytes 368672 | tf_op jit(solution)/shard_map/ppermute | solution.py:25
  214.9 9.2 %collective-permute-done.7 = bf16[1,1,720,256]{3,2,1,0:T(8,128)(2,1)S(1)} collective-permute-done((bf16[1,1,720,256]{3,2,1,0:T(8,128)(2,1)S(1)}, bf16[1,1,720,256]{3,2,1,0:T(8,128)(2,1)S(1)}, u32[]{:S(2)}, u32[]{:S(2)}) %collective-permute-start.7) | collective-permute-done | bytes 368672 | tf_op jit(solution)/shard_map/ppermute | solution.py:28
  224.2 1.2 fusion.13
  225.4 0.1 fusion.12
  225.5 0.9 convert_element_type.127
  226.4 0.9 copy.90
  227.3 1.4 copy.91
  (77 shorter events, 0.7 us)
Async XLA Ops:
  0.6 15.9 %copy-start.4 = (bf16[1,2,720,256]{3,2,1,0:T(8,128)(2,1)S(1)}, bf16[1,2,720,256]{3,2,1,0:T(8,128)(2,1)}, u32[]{:S(2)}) copy-start(bf16[1,2,720,256]{3,2,1,0:T(8,128)(2,1)} %param.24) | copy-start | bytes 2211844
  1.9 14.7 %collective-permute-start.1 = (bf16[1,1,720,256]{3,2,1,0:T(8,128)(2,1)S(1)}, bf16[1,1,720,256]{3,2,1,0:T(8,128)(2,1)S(1)}, u32[]{:S(2)}, u32[]{:S(2)}) collective-permute-start(bf16[1,1,720,256]{3,2,1,0:T(8,128)(2,1)S(1)} %get-tuple-element.143), channel_id=1, source_target_pairs={{8,0},{16,8},{24,16},{9,1},{17,9},{25,17},{10,2},{18,10},{26,18},{... | collective-permute-start | bytes 1105928 | tf_op jit(solution)/shard_map/ppermute | solution.py:28
  3.2 13.3 %collective-permute-start = (bf16[1,1,720,256]{3,2,1,0:T(8,128)(2,1)S(1)}, bf16[1,1,720,256]{3,2,1,0:T(8,128)(2,1)S(1)}, u32[]{:S(2)}, u32[]{:S(2)}) collective-permute-start(bf16[1,1,720,256]{3,2,1,0:T(8,128)(2,1)S(1)} %get-tuple-element.144), channel_id=1, source_target_pairs={{0,8},{8,16},{16,24},{1,9},{9,17},{17,25},{2,10},{10,18},{18,26},{... | collective-permute-start | bytes 1105928 | tf_op jit(solution)/shard_map/ppermute | solution.py:25
  11.1 5.5 %copy-start.12 = (f32[3]{0:T(128)}, f32[3]{0:T(128)S(1)}, u32[]{:S(2)}) copy-start(f32[3]{0:T(128)S(1)} %pad.47.clone) | copy-start | bytes 40
  11.3 5.4 %copy-start.8 = (f32[1,720]{1,0:T(1,128)}, f32[1,720]{1,0:T(1,128)S(1)}, u32[]{:S(2)}) copy-start(f32[1,720]{1,0:T(1,128)S(1)} %get-tuple-element.156) | copy-start | bytes 8644
  11.3 5.4 %copy-start.10 = (f32[1,720]{1,0:T(1,128)}, f32[1,720]{1,0:T(1,128)S(1)}, u32[]{:S(2)}) copy-start(f32[1,720]{1,0:T(1,128)S(1)} %get-tuple-element.157) | copy-start | bytes 8644
  20.9 2.5 %collective-permute-start.2 = (bf16[1,4,16,256]{3,2,1,0:T(8,128)(2,1)S(1)}, bf16[1,4,16,256]{3,2,1,0:T(8,128)(2,1)S(1)}, u32[]{:S(2)}, u32[]{:S(2)}) collective-permute-start(bf16[1,4,16,256]{3,2,1,0:T(8,128)(2,1)S(1)} %get-tuple-element.141), channel_id=1, source_target_pairs={{0,4},{4,0},{1,5},{5,1},{2,6},{6,2},{3,7},{7,3},{8,12},{12,8},{9,1... | collective-permute-start | bytes 98312 | tf_op jit(solution)/shard_map/ppermute | solution.py:25
  21.3 2.1 collective-permute-start.3
  22.8 1.6 copy-start.6
  34.1 3.7 %copy-start = (bf16[9,256,256]{2,1,0:T(8,128)(2,1)S(1)}, bf16[9,256,256]{2,1,0:T(8,128)(2,1)}, u32[]{:S(2)}) copy-start(bf16[9,256,256]{2,1,0:T(8,128)(2,1)} %weight.1) | copy-start | bytes 3538948
  34.1 3.7 %copy-start.1 = (bf16[2,720,256]{2,1,0:T(8,128)(2,1)S(1)}, bf16[2,720,256]{2,1,0:T(8,128)(2,1)}, u32[]{:S(2)}) copy-start(bf16[2,720,256]{2,1,0:T(8,128)(2,1)} %target.1) | copy-start | bytes 2211844
  159.8 14.3 %copy-start.2 = (bf16[1,2,9,720,256]{4,3,2,1,0:T(8,128)(2,1)S(1)}, bf16[1,2,9,720,256]{4,3,2,1,0:T(8,128)(2,1)}, u32[]{:S(2)}) copy-start(bf16[1,2,9,720,256]{4,3,2,1,0:T(8,128)(2,1)} %get-tuple-element.135) | copy-start | bytes 19906564
  170.9 8.9 %copy-start.7 = (f32[720,752]{1,0:T(8,128)S(1)}, f32[720,752]{1,0:T(8,128)}, u32[]{:S(2)}) copy-start(f32[720,752]{1,0:T(8,128)} %subtract_convert_fusion) | copy-start | bytes 6497284
  191.7 5.8 %copy-start.9 = (f32[1,720]{1,0:T(1,128)S(1)}, f32[1,720]{1,0:T(1,128)}, u32[]{:S(2)}) copy-start(f32[1,720]{1,0:T(1,128)} %copy-done.8) | copy-start | bytes 8644
  191.7 5.8 %copy-start.11 = (f32[1,720]{1,0:T(1,128)S(1)}, f32[1,720]{1,0:T(1,128)}, u32[]{:S(2)}) copy-start(f32[1,720]{1,0:T(1,128)} %copy-done.10) | copy-start | bytes 8644
  191.7 5.8 %copy-start.13 = (f32[3]{0:T(128)S(1)}, f32[3]{0:T(128)}, u32[]{:S(2)}) copy-start(f32[3]{0:T(128)} %copy-done.12) | copy-start | bytes 40
  200.1 1.3 collective-permute-start.4
  200.3 1.2 collective-permute-start.5
  201.6 1.6 copy-start.3
  203.2 11.7 %collective-permute-start.6 = (bf16[1,1,720,256]{3,2,1,0:T(8,128)(2,1)S(1)}, bf16[1,1,720,256]{3,2,1,0:T(8,128)(2,1)S(1)}, u32[]{:S(2)}, u32[]{:S(2)}) collective-permute-start(bf16[1,1,720,256]{3,2,1,0:T(8,128)(2,1)S(1)} %get-tuple-element.139), channel_id=1, source_target_pairs={{0,8},{8,16},{16,24},{1,9},{9,17},{17,25},{2,10},{10,18},{18,26},{... | collective-permute-start | bytes 1105928 | tf_op jit(solution)/shard_map/ppermute | solution.py:25
  206.6 17.5 %collective-permute-start.7 = (bf16[1,1,720,256]{3,2,1,0:T(8,128)(2,1)S(1)}, bf16[1,1,720,256]{3,2,1,0:T(8,128)(2,1)S(1)}, u32[]{:S(2)}, u32[]{:S(2)}) collective-permute-start(bf16[1,1,720,256]{3,2,1,0:T(8,128)(2,1)S(1)} %get-tuple-element.140), channel_id=1, source_target_pairs={{8,0},{16,8},{24,16},{9,1},{17,9},{25,17},{10,2},{18,10},{26,18},{... | collective-permute-start | bytes 1105928 | tf_op jit(solution)/shard_map/ppermute | solution.py:28
  225.3 2.0 copy-start.5

commit v2 on v1

--- a/solution.py
+++ b/solution.py
@@ -384,6 +384,19 @@
     return response, feature_grad, weight_sum * scale, loss
 
 
+def lon_sum(value):
+    if lax.axis_size("lon") == 2:
+        return value + lax.ppermute(value, "lon", [(0, 1), (1, 0)])
+    return lax.psum(value, "lon")
+
+
+def lat_swap(down, up):
+    count = lax.axis_size("lat")
+    forward = [(i, i + 1) for i in range(count - 1)]
+    backward = [(target, source) for source, target in forward]
+    return lax.ppermute(down, "lat", backward), lax.ppermute(up, "lat", forward)
+
+
 def per_device(inputs, weight, spread, target):
     ens_local, row_count, lon_count, channels = inputs.shape
     reach = HMAX
@@ -396,22 +409,32 @@
     kernels = kernel_rows(spread, lon_count, reach)
     local_basis = circle_basis(lon_first, lon_count, lon_total)
     extended = extended_2(inputs, (("lat", 1),), 1, False)
-    window = extended_2(extended, (("lon", 2),), reach, True)
     local_sums = jnp.einsum(
         "pj,erjc->eprc", local_basis, extended.astype(jnp.float32), precision=highest
     )
-    circle_sums = lax.psum(local_sums, "lon")
-    banded = jnp.concatenate(
+    circle_sums = lon_sum(local_sums)
+    own = extended_2(inputs, (("lon", 2),), reach, True)
+    edge_rows = jnp.concatenate([extended[:, :1], extended[:, row_count + 1 :]], 1)
+    beyond = extended_2(edge_rows, (("lon", 2),), reach, True)
+
+    def banded_row(row, lat_tap):
+        source = row + lat_tap - 1
+        if source < 0:
+            strip = beyond[:, 0]
+        elif source >= row_count:
+            strip = beyond[:, 1]
+        else:
+            strip = own[:, source]
+        return jnp.einsum(
+            "bjq,eqc->ebjc", kernels[row], strip, preferred_element_type=jnp.float32
+        )
+
+    banded = jnp.stack(
         [
-            jnp.einsum(
-                "objq,eoqc->eobjc",
-                kernels,
-                window[:, lat_tap : lat_tap + row_count],
-                preferred_element_type=jnp.float32,
-            )
-            for lat_tap in range(3)
+            jnp.concatenate([banded_row(row, lat_tap) for lat_tap in range(3)], 1)
+            for row in range(row_count)
         ],
-        2,
+        1,
     )
     rounds = circular(circle_sums, local_basis, lon_total, row_count)
     features = jnp.where(polar_mask, rounds, banded).astype(jnp.bfloat16)
@@ -428,57 +451,66 @@
         response, feature_grad, grad_weight, loss = plain_middle(
             features, weight, target, lat_weight, scale, lat_total * lon_total * channels
         )
-    zero_grad = jnp.zeros_like(feature_grad)
-    band_grad = jnp.where(polar_mask, zero_grad, feature_grad)
-    circle_grad = jnp.where(polar_mask, feature_grad, zero_grad)
-    window_grad = jnp.zeros(
-        (ens_local, row_count + 2, lon_count + 2 * reach, channels), jnp.float32
-    )
-    sum_grad = jnp.zeros((ens_local, 3, row_count + 2, channels), jnp.float32)
-    cos_wave = local_basis[1]
-    sin_wave = local_basis[2]
-    for lat_tap in range(3):
-        picked = band_grad[:, :, 3 * lat_tap : 3 * lat_tap + 3]
-        window_grad = window_grad.at[:, lat_tap : lat_tap + row_count].add(
-            jnp.einsum("objq,eobjc->eoqc", kernels, picked, preferred_element_type=jnp.float32)
-        )
-        tap_grad = circle_grad[:, :, 3 * lat_tap : 3 * lat_tap + 3].astype(jnp.float32)
-        mean_grad = jnp.sum(tap_grad[:, :, 0], axis=2) / lon_total
-        cos_grad = (
-            2.0
-            / lon_total
-            * (
-                jnp.einsum("j,eojc->eoc", cos_wave, tap_grad[:, :, 1], precision=highest)
-                - jnp.einsum("j,eojc->eoc", sin_wave, tap_grad[:, :, 2], precision=highest)
-            )
-        )
-        sin_grad = (
-            2.0
-            / lon_total
-            * (
-                jnp.einsum("j,eojc->eoc", sin_wave, tap_grad[:, :, 1], precision=highest)
-                + jnp.einsum("j,eojc->eoc", cos_wave, tap_grad[:, :, 2], precision=highest)
-            )
-        )
-        sum_grad = sum_grad.at[:, :, lat_tap : lat_tap + row_count].add(
-            jnp.stack([mean_grad, cos_grad, sin_grad], 1)
-        )
-    sum_total = lax.psum(sum_grad, "lon")
-    core = window_grad[:, :, reach : reach + lon_count] + jnp.einsum(
-        "pj,eprc->erjc", local_basis, sum_total, precision=highest
-    )
+    band_kernels = jnp.where(polar_rows[:, None, None, None], 0.0, kernels).astype(jnp.bfloat16)
+    high = local_basis.astype(jnp.bfloat16)
+    low = (local_basis - high.astype(jnp.float32)).astype(jnp.bfloat16)
+    waves = jnp.einsum(
+        "pj,eokjc->eokpc",
+        jnp.concatenate([high, low]),
+        feature_grad,
+        preferred_element_type=jnp.float32,
+    )
+    waves = waves[:, :, :, :3] + waves[:, :, :, 3:]
+    waves = jnp.where(polar_mask, waves, 0.0)
+
+    def circle_row(row, lat_tap):
+        taps = waves[:, row, 3 * lat_tap : 3 * lat_tap + 3]
+        mean_grad = taps[:, 0, 0] / lon_total
+        cos_grad = 2.0 / lon_total * (taps[:, 1, 1] - taps[:, 2, 2])
+        sin_grad = 2.0 / lon_total * (taps[:, 1, 2] + taps[:, 2, 1])
+        return jnp.stack([mean_grad, cos_grad, sin_grad], 1)
+
+    def band_row(row, lat_tap):
+        return jnp.einsum(
+            "bjq,ebjc->eqc",
+            band_kernels[row],
+            feature_grad[:, row, 3 * lat_tap : 3 * lat_tap + 3],
+            preferred_element_type=jnp.float32,
+        )
+
+    last = row_count - 1
+    down_window, up_window = lat_swap(
+        band_row(0, 0).astype(jnp.bfloat16), band_row(last, 2).astype(jnp.bfloat16)
+    )
+    down_sums, up_sums = lat_swap(circle_row(0, 0), circle_row(last, 2))
+    sum_rows, window_rows = [], []
+    for source in range(row_count):
+        pairs = [(row, source - row + 1) for row in range(row_count) if 0 <= source - row + 1 <= 2]
+        sums = sum(circle_row(*pair) for pair in pairs)
+        window = sum(band_row(*pair) for pair in pairs)
+        if source == 0:
+            sums, window = sums + up_sums, window + up_window.astype(jnp.float32)
+        if source == last:
+            sums, window = sums + down_sums, window + down_window.astype(jnp.float32)
+        sum_rows.append(sums)
+        window_rows.append(window)
+    sum_total = lon_sum(jnp.stack(sum_rows, 2))
+    window_grad = jnp.stack(window_rows, 1)
+    circle_part = sum(
+        local_basis[p][None, None, :, None] * sum_total[:, p][:, :, None, :] for p in range(3)
+    )
+    core = window_grad[:, :, reach : reach + lon_count] + circle_part
     rims = jnp.concatenate([window_grad[:, :, :reach], window_grad[:, :, reach + lon_count :]], 2)
     arrived = extended_2(rims.astype(jnp.bfloat16), (("lon", 2),), reach, True).astype(rims.dtype)
-    core = core.at[:, :, :reach].add(arrived[:, :, :reach])
-    core = core.at[:, :, lon_count - reach :].add(arrived[:, :, 3 * reach :])
-    edges = jnp.concatenate([core[:, :1], core[:, row_count + 1 :]], 1)
-    arrived_rows = extended_2(edges.astype(jnp.bfloat16), (("lat", 1),), 1, False).astype(
-        edges.dtype
-    )
-    inner = core[:, 1 : row_count + 1]
-    inner = inner.at[:, 0].add(arrived_rows[:, 0])
-    inner = inner.at[:, row_count - 1].add(arrived_rows[:, 3])
-    return (response, inner.astype(jnp.bfloat16), grad_weight, loss)
+    core = jnp.concatenate(
+        [
+            core[:, :, :reach] + arrived[:, :, :reach],
+            core[:, :, reach : lon_count - reach],
+            core[:, :, lon_count - reach :] + arrived[:, :, 3 * reach :],
+        ],
+        2,
+    )
+    return (response, core.astype(jnp.bfloat16), grad_weight, loss)
 
 
 def solution(mesh):

time: 231 us -> 186 us (0.81)
  matrix products: 45.9 us -> 22.9 us
  waiting for transfers between devices: 19.5 us -> 9.97 us
  blocking collectives: 7.13 us -> 0 us
  Pallas kernels: 113 us -> 106 us
  starting transfers between devices: 12.6 us -> 19.3 us
  other arithmetic: 19.9 us -> 15.7 us
  local copies, waits for them, and re-layouts: 8.35 us -> 5.71 us
    dot_general x19 -> x13, matrix products: 45.2 us -> 22.1 us  [the longest x6 14.9 us: band_row(): jnp.einsum('bjq,ebjc->eqc', band_kernels[row], feature_grad[:, row, 3 * l...]
    ppermute x0 -> x6, starting transfers between devices: none -> 11.4 us  [the longest x2 8.78 us: lat_swap(): lax.ppermute(up, 'lat', forward)]
    ppermute x4, waiting for transfers between devices: 10.1 us -> 0.24 us  [extended_2(): lax.ppermute(lax.slice_in_dim(block, block.shape[dim] - width, None, axis...]
    pallas_call x1, Pallas kernels: 113 us -> 106 us  [run_middle(): pl.pallas_call(functools.partial(middle, scale), out_shape=[shape((rows,...]
    psum x2 -> x0, blocking collectives: 7.13 us -> none  [the longest x1 3.77 us: per_device(): sum_total = lax.psum(sum_grad, 'lon')]
    ppermute x0 -> x6, waiting for transfers between devices: none -> 6.56 us  [the longest x2 6.1 us: lat_swap(): lax.ppermute(down, 'lat', backward)]
    ppermute x4, waiting for transfers between devices: 9.39 us -> 3.16 us  [extended_2(): lax.ppermute(lax.slice_in_dim(block, 0, width, axis=dim), axis, backward)]
    select_n x1 -> x2, other arithmetic: 8.55 us -> 3.57 us  [the longest x1 3.48 us: per_device(): jnp.where(polar_rows[:, None, None, None], 0.0, kernels)]
  transfers between devices with their start and end apart: 8 -> 14, of which waited for: 5 -> 5; matrix products, arithmetic and copies ran while one was open for 3% -> 11% of each run, Pallas kernels for 0% -> 0%
where the time goes in v2:
time: 186 us; the launch traced here: 183 us
  Pallas kernels  106 us (57%)
  matrix products  22.9 us (12%)
  starting transfers between devices  19.3 us (10%)
  other arithmetic  15.7 us (8%)
  waiting for transfers between devices  9.97 us (5%)
  local copies, waits for them, and re-layouts  5.71 us (3%)
  between operations  3.12 us (2%)
    pallas_call x1, Pallas kernels, run_middle(): pl.pallas_call(functools.partial(middle, scale), out_shape=[shape((rows,...  106 us
    dot_general x6, matrix products, band_row(): jnp.einsum('bjq,ebjc->eqc', band_kernels[row], feature_grad[:, row, 3 * l...  14.9 us
    ppermute x2, starting transfers between devices, lat_swap(): lax.ppermute(up, 'lat', forward)  8.78 us
    dot_general x6, matrix products, banded_row(): jnp.einsum('bjq,eqc->ebjc', kernels[row], strip, preferred_element_type=j...  6.3 us
    ppermute x2, waiting for transfers between devices, lat_swap(): lax.ppermute(down, 'lat', backward)  6.1 us
    ppermute x4, starting transfers between devices, extended_2(): lax.ppermute(lax.slice_in_dim(block, block.shape[dim] - width, None, axis...  5.5 us
    convert_element_type x1, other arithmetic, per_device(): features = jnp.where(polar_mask, rounds, banded).astype(jnp.bfloat16)  3.96 us
  transfers between devices with their start and end apart: 14, of which 5 were waited for; matrix products, arithmetic and copies ran while one was open for 11% of the time, Pallas kernels for 0%

profile of v2, /device:TPU:0, one launch (start us, length us, event | category | flops | bytes accessed | tf_op | source)
XLA Modules:
  0.0 182.8 jit_solution(14637734282083016853)
XLA Ops:
  0.6 1.9 %fusion.96 = (bf16[1,1,720,256]{3,2,1,0:T(8,128)(2,1)}, bf16[1,1,720,256]{3,2,1,0:T(8,128)(2,1)S(1)}) fusion(bf16[1,2,720,256]{3,2,1,0:T(8,128)(2,1)} %param.4), kind=kLoop, calls=%fused_computation.203 | loop fusion | bytes 1474560 | tf_op jit(solution)/shard_map/slice | solution.py:26
  2.5 4.9 %collective-permute-start = (bf16[1,1,720,256]{3,2,1,0:T(8,128)(2,1)}, bf16[1,1,720,256]{3,2,1,0:T(8,128)(2,1)S(1)}, u32[]{:S(2)}, u32[]{:S(2)}) collective-permute-start(bf16[1,1,720,256]{3,2,1,0:T(8,128)(2,1)} %get-tuple-element.20), channel_id=1, source_target_pairs={{0,8},{8,16},{16,24},{1,9},{9,17},{17,25},{2,10},{10,18},{18,26},{... | collective-permute-start | bytes 1105928 | tf_op jit(solution)/shard_map/ppermute | solution.py:25
  7.4 1.3 collective-permute-start.1
  8.7 0.7 fusion.94
  9.4 0.5 collective-permute-start.6
  9.9 0.1 fusion.58
  10.1 0.1 fusion.50
  10.2 0.1 subtract_convert_fusion.1
  10.3 0.7 convert_multiply_fusion.2
  10.9 0.2 subtract_convert_fusion
  11.2 0.1 broadcast_multiply_fusion
  11.2 3.1 %divide_convert_fusion = bf16[2,3,720,752]{3,2,1,0:T(8,128)(2,1)S(1)} fusion(f32[2]{0:T(128)S(1)} %convert_multiply_fusion.2, f32[2,3]{1,0:T(2,128)S(1)} %broadcast_multiply_fusion, f32[720,752]{1,0:T(8,128)S(1)} %subtract_convert_fusion), kind=kLoop, calls=%fused_computation.2 | loop fusion | flops 22740480 | bytes 8663072 | tf_op jit(solution)/shard_map/convert_element_type | solution.py:40
  14.4 3.5 %broadcast_select_fusion = bf16[2,3,720,752]{3,2,1,0:T(8,128)(2,1)S(1)} fusion(pred[2]{0:T(512)(128)(4,1)S(1)} %compare_or_fusion, f32[2]{0:T(128)S(1)} %convert_multiply_fusion.2, f32[2,3]{1,0:T(2,128)S(1)} %broadcast_multiply_fusion, f32[720,752]{1,0:T(8,128)S(1)} %subtract_convert_fusion), kind=kLoop, calls=%fused_computation.3 | loop fusion | flops 25989120 | bytes 8663074 | tf_op jit(solution)/shard_map/jit(_where)/select_n | solution.py:454
  17.9 0.1 constant_dynamic-update-slice_fusion.3
  18.0 1.0 fusion.13
  19.1 1.1 fusion.14
  20.1 1.1 fusion.17
  21.2 1.0 fusion.18
  22.2 3.0 %collective-permute-done.1 = bf16[1,1,720,256]{3,2,1,0:T(8,128)(2,1)S(1)} collective-permute-done((bf16[1,1,720,256]{3,2,1,0:T(8,128)(2,1)S(1)}, bf16[1,1,720,256]{3,2,1,0:T(8,128)(2,1)S(1)}, u32[]{:S(2)}, u32[]{:S(2)}) %collective-permute-start.1) | collective-permute-done | bytes 368672 | tf_op jit(solution)/shard_map/ppermute | solution.py:28
  25.2 0.8 fusion.40
  26.1 0.6 collective-permute-start.3
  26.7 0.1 collective-permute-start.4
  26.7 0.5 collective-permute-done.2
  27.3 0.1 broadcast_dynamic-update-slice_fusion.2
  27.3 0.3 multiply_dynamic-update-slice_fusion.5
  27.6 0.3 multiply_dynamic-update-slice_fusion.4
  27.9 0.1 broadcast_dynamic-update-slice_fusion.1
  28.0 0.3 multiply_dynamic-update-slice_fusion.3
  28.3 0.3 multiply_dynamic-update-slice_fusion.2
  28.6 0.1 broadcast_dynamic-update-slice_fusion
  28.7 0.3 multiply_dynamic-update-slice_fusion.1
  29.0 0.3 multiply_dynamic-update-slice_fusion
  29.3 0.1 pad_maximum_fusion
  29.3 1.1 fusion.15
  30.4 1.1 fusion.16
  31.5 0.0 copy-start.1
  31.5 4.0 %fusion.feat = bf16[2,9,720,256]{3,2,1,0:T(8,128)(2,1)} fusion(bf16[2,9,720,256]{3,2,1,0:T(8,128)(2,1)S(1)} %multiply_dynamic-update-slice_fusion, bf16[1,3,720,256]{3,2,1,0:T(8,128)(2,1)S(1)} %fusion.15, bf16[1,3,720,256]{3,2,1,0:T(8,128)(2,1)S(1)} %fusion.14, bf16[1,3,720,256]{3,2,1,0:T(8,128)(2,1)S(1)} %fusion.13, bf16[1,3,720,256]{3,2,1,0:T(8,128)(2,1)S(1)} %fusion.18, ...), kind=kLoop, calls=%fused_computation.1 | loop fusion | flops 19906560 | bytes 19906562 | tf_op jit(solution)/shard_map/convert_element_type | solution.py:440
  35.4 0.1 broadcast_in_dim.52.row_weight
  35.5 106.1 %middle.1 = (bf16[2,720,256]{2,1,0:T(8,128)(2,1)S(1)}, bf16[2,9,720,256]{3,2,1,0:T(8,128)(2,1)}, f32[9,256,256]{2,1,0:T(8,128)}, f32[8,128]{1,0:T(8,128)S(1)}) custom-call(bf16[2,9,720,256]{3,2,1,0:T(8,128)(2,1)} %fusion.feat, bf16[9,256,256]{2,1,0:T(8,128)(2,1)S(1)} %copy-done, bf16[2,720,256]{2,1,0:T(8,128)(2,1)S(1)} %copy-done.1, ...), custom_call_target="tpu_custom_call" | custom-call | tf_op jit(solution)/shard_map/middle/pallas_call | solution.py:328
  141.7 2.9 %fusion.39 = bf16[1,752,256]{2,1,0:T(8,128)(2,1)S(1)} fusion(bf16[2,3,720,752]{3,2,1,0:T(8,128)(2,1)S(1)} %broadcast_select_fusion, bf16[1,2,9,720,256]{4,3,2,1,0:T(8,128)(2,1)} %bitcast.303), kind=kOutput, calls=%fused_computation.59 | convolution fusion | flops 831844352 | bytes 4808704 | tf_op jit(solution)/shard_map/bjq,ebjc->eqc/dot_general | solution.py:474
  144.5 0.3 copy-done.4
  144.9 2.4 %fusion.28 = f32[256,752]{0,1:T(8,128)} fusion(bf16[2,3,720,752]{3,2,1,0:T(8,128)(2,1)S(1)} %broadcast_select_fusion, bf16[1,2,9,720,256]{4,3,2,1,0:T(8,128)(2,1)S(1)} %bitcast.306), kind=kOutput, calls=%fused_computation.48 | convolution fusion | flops 831651840 | bytes 5193728 | tf_op jit(solution)/shard_map/bjq,ebjc->eqc/dot_general | solution.py:474
  147.2 1.5 fusion.26
  148.7 1.5 fusion.38
  150.2 1.0 convolution_bitcast_fusion
  151.2 0.1 fusion.41
  151.3 3.4 %collective-permute-start.9 = (f32[1,3,256]{2,0,1:T(1,128)S(1)}, f32[1,3,256]{2,0,1:T(1,128)S(1)}, u32[]{:S(2)}, u32[]{:S(2)}) collective-permute-start(f32[1,3,256]{2,0,1:T(1,128)S(1)} %pad_maximum_fusion.8), channel_id=1, source_target_pairs={{0,8},{8,16},{16,24},{1,9},{9,17},{17,25},{2,10},{10,18},{18,26},{... | collective-permute-start | bytes 9224 | tf_op jit(solution)/shard_map/ppermute | solution.py:397
  154.8 1.3 collective-permute-start.10
  156.1 1.3 collective-permute-start.8
  157.4 5.4 %collective-permute-start.7 = (bf16[1,752,256]{2,1,0:T(8,128)(2,1)S(1)}, bf16[1,752,256]{2,1,0:T(8,128)(2,1)S(1)}, u32[]{:S(2)}, u32[]{:S(2)}) collective-permute-start(bf16[1,752,256]{2,1,0:T(8,128)(2,1)S(1)} %fusion.38), channel_id=1, source_target_pairs={{0,8},{8,16},{16,24},{1,9},{9,17},{17,25},{2,10},{10,18},{18,26},{... | collective-permute-start | bytes 1155080 | tf_op jit(solution)/shard_map/ppermute | solution.py:397
  162.9 0.1 collective-permute-start.11
  163.0 0.6 slice_reduce_fusion
  164.3 6.1 %collective-permute-done.8 = bf16[1,752,256]{2,1,0:T(8,128)(2,1)S(1)} collective-permute-done((bf16[1,752,256]{2,1,0:T(8,128)(2,1)S(1)}, bf16[1,752,256]{2,1,0:T(8,128)(2,1)S(1)}, u32[]{:S(2)}, u32[]{:S(2)}) %collective-permute-start.8) | collective-permute-done | bytes 385056 | tf_op jit(solution)/shard_map/ppermute | solution.py:397
  170.4 3.9 %add_bitcast_fusion = f32[1,1,752,256]{3,2,1,0:T(8,128)S(1)} fusion(bf16[1,752,256]{2,1,0:T(8,128)(2,1)S(1)} %collective-permute-done.8, f32[256,752]{0,1:T(8,128)} %fusion.28, bf16[2,3,720,752]{3,2,1,0:T(8,128)(2,1)} %copy-done.2, bf16[1,2,9,720,256]{4,3,2,1,0:T(8,128)(2,1)} %bitcast.304), kind=kOutput, calls=%fused_computation.69 | convolution fusion | flops 832229376 | bytes 6348800 | tf_op jit(solution)/shard_map/bjq,ebjc->eqc/dot_general | solution.py:474
  174.3 2.7 %add_bitcast_fusion.1 = f32[1,1,752,256]{3,2,1,0:T(8,128)S(1)} fusion(bf16[1,752,256]{2,1,0:T(8,128)(2,1)S(1)} %collective-permute-done.7, f32[256,752]{0,1:T(8,128)S(1)} %fusion.26, bf16[2,3,720,752]{3,2,1,0:T(8,128)(2,1)S(1)} %copy-done.3, bf16[1,2,9,720,256]{4,3,2,1,0:T(8,128)(2,1)} %bitcast.305), kind=kOutput, calls=%fused_computation.70 | convolution fusion | flops 832229376 | bytes 6348800 | tf_op jit(solution)/shard_map/bjq,ebjc->eqc/dot_general | solution.py:474
  177.1 0.1 collective-permute-start.12
  177.2 0.5 collective-permute-start.13
  177.7 0.3 fusion.20
  178.0 0.1 slice.656
  178.1 0.2 collective-permute-done.12
  178.3 0.2 collective-permute-done.13
  178.5 0.9 pad_maximum_fusion.1
  179.4 0.9 copy.49
  180.3 1.4 copy.50
  (63 shorter events, 0.4 us)
Async XLA Ops:
  2.5 19.7 %collective-permute-start = (bf16[1,1,720,256]{3,2,1,0:T(8,128)(2,1)}, bf16[1,1,720,256]{3,2,1,0:T(8,128)(2,1)S(1)}, u32[]{:S(2)}, u32[]{:S(2)}) collective-permute-start(bf16[1,1,720,256]{3,2,1,0:T(8,128)(2,1)} %get-tuple-element.20), channel_id=1, source_target_pairs={{0,8},{8,16},{16,24},{1,9},{9,17},{17,25},{2,10},{10,18},{18,26},{... | collective-permute-start | bytes 1105928 | tf_op jit(solution)/shard_map/ppermute | solution.py:25
  7.4 17.9 %collective-permute-start.1 = (bf16[1,1,720,256]{3,2,1,0:T(8,128)(2,1)S(1)}, bf16[1,1,720,256]{3,2,1,0:T(8,128)(2,1)S(1)}, u32[]{:S(2)}, u32[]{:S(2)}) collective-permute-start(bf16[1,1,720,256]{3,2,1,0:T(8,128)(2,1)S(1)} %get-tuple-element.21), channel_id=1, source_target_pairs={{8,0},{16,8},{24,16},{9,1},{17,9},{25,17},{10,2},{18,10},{26,18},{... | collective-permute-start | bytes 1105928 | tf_op jit(solution)/shard_map/ppermute | solution.py:28
  9.4 8.5 %collective-permute-start.5 = (bf16[1,2,16,256]{3,2,1,0:T(8,128)(2,1)S(1)}, bf16[1,2,16,256]{3,2,1,0:T(8,128)(2,1)S(1)}, u32[]{:S(2)}, u32[]{:S(2)}) collective-permute-start(bf16[1,2,16,256]{3,2,1,0:T(8,128)(2,1)S(1)} %get-tuple-element.17), channel_id=1, source_target_pairs={{0,4},{4,0},{1,5},{5,1},{2,6},{6,2},{3,7},{7,3},{8,12},{12,8},{9,1... | collective-permute-start | bytes 49160 | tf_op jit(solution)/shard_map/ppermute | solution.py:25
  9.4 8.6 %collective-permute-start.6 = (bf16[1,2,16,256]{3,2,1,0:T(8,128)(2,1)S(1)}, bf16[1,2,16,256]{3,2,1,0:T(8,128)(2,1)S(1)}, u32[]{:S(2)}, u32[]{:S(2)}) collective-permute-start(bf16[1,2,16,256]{3,2,1,0:T(8,128)(2,1)S(1)} %get-tuple-element.16), channel_id=1, source_target_pairs={{4,0},{0,4},{5,1},{1,5},{6,2},{2,6},{7,3},{3,7},{12,8},{8,12},{13,... | collective-permute-start | bytes 49160 | tf_op jit(solution)/shard_map/ppermute | solution.py:28
  14.3 3.6 %copy-start.5 = (bf16[1,2,720,256]{3,2,1,0:T(8,128)(2,1)S(1)}, bf16[1,2,720,256]{3,2,1,0:T(8,128)(2,1)}, u32[]{:S(2)}) copy-start(bf16[1,2,720,256]{3,2,1,0:T(8,128)(2,1)} %param.4) | copy-start | bytes 2211844
  17.8 130.9 %copy-start.2 = (bf16[2,3,720,752]{3,2,1,0:T(8,128)(2,1)}, bf16[2,3,720,752]{3,2,1,0:T(8,128)(2,1)S(1)}, u32[]{:S(2)}) copy-start(bf16[2,3,720,752]{3,2,1,0:T(8,128)(2,1)S(1)} %broadcast_select_fusion) | copy-start | bytes 19491844
  26.0 1.2 collective-permute-start.2
  26.1 3.2 %collective-permute-start.3 = (bf16[1,2,16,256]{3,2,1,0:T(8,128)(2,1)S(1)}, bf16[1,2,16,256]{3,2,1,0:T(8,128)(2,1)S(1)}, u32[]{:S(2)}, u32[]{:S(2)}) collective-permute-start(bf16[1,2,16,256]{3,2,1,0:T(8,128)(2,1)S(1)} %get-tuple-element.18), channel_id=1, source_target_pairs={{0,4},{4,0},{1,5},{5,1},{2,6},{6,2},{3,7},{7,3},{8,12},{12,8},{9,1... | collective-permute-start | bytes 49160 | tf_op jit(solution)/shard_map/ppermute | solution.py:25
  26.7 2.6 %collective-permute-start.4 = (bf16[1,2,16,256]{3,2,1,0:T(8,128)(2,1)S(1)}, bf16[1,2,16,256]{3,2,1,0:T(8,128)(2,1)S(1)}, u32[]{:S(2)}, u32[]{:S(2)}) collective-permute-start(bf16[1,2,16,256]{3,2,1,0:T(8,128)(2,1)S(1)} %get-tuple-element.19), channel_id=1, source_target_pairs={{4,0},{0,4},{5,1},{1,5},{6,2},{2,6},{7,3},{3,7},{12,8},{8,12},{13,... | collective-permute-start | bytes 49160 | tf_op jit(solution)/shard_map/ppermute | solution.py:28
  31.5 4.1 %copy-start = (bf16[9,256,256]{2,1,0:T(8,128)(2,1)S(1)}, bf16[9,256,256]{2,1,0:T(8,128)(2,1)}, u32[]{:S(2)}) copy-start(bf16[9,256,256]{2,1,0:T(8,128)(2,1)} %weight.1) | copy-start | bytes 3538948
  31.5 4.0 %copy-start.1 = (bf16[2,720,256]{2,1,0:T(8,128)(2,1)S(1)}, bf16[2,720,256]{2,1,0:T(8,128)(2,1)}, u32[]{:S(2)}) copy-start(bf16[2,720,256]{2,1,0:T(8,128)(2,1)} %target.1) | copy-start | bytes 2211844
  141.6 3.2 %copy-start.4 = (bf16[2,9,720,256]{3,2,1,0:T(8,128)(2,1)S(1)}, bf16[2,9,720,256]{3,2,1,0:T(8,128)(2,1)}, u32[]{:S(2)}) copy-start(bf16[2,9,720,256]{3,2,1,0:T(8,128)(2,1)} %get-tuple-element.9) | copy-start | bytes 19906564
  151.3 11.5 %collective-permute-start.9 = (f32[1,3,256]{2,0,1:T(1,128)S(1)}, f32[1,3,256]{2,0,1:T(1,128)S(1)}, u32[]{:S(2)}, u32[]{:S(2)}) collective-permute-start(f32[1,3,256]{2,0,1:T(1,128)S(1)} %pad_maximum_fusion.8), channel_id=1, source_target_pairs={{0,8},{8,16},{16,24},{1,9},{9,17},{17,25},{2,10},{10,18},{18,26},{... | collective-permute-start | bytes 9224 | tf_op jit(solution)/shard_map/ppermute | solution.py:397
  154.8 8.1 %collective-permute-start.10 = (f32[1,3,256]{2,0,1:T(1,128)S(1)}, f32[1,3,256]{2,0,1:T(1,128)S(1)}, u32[]{:S(2)}, u32[]{:S(2)}) collective-permute-start(f32[1,3,256]{2,0,1:T(1,128)S(1)} %pad_maximum_fusion.9), channel_id=1, source_target_pairs={{8,0},{16,8},{24,16},{9,1},{17,9},{25,17},{10,2},{18,10},{26,18},{... | collective-permute-start | bytes 9224 | tf_op jit(solution)/shard_map/ppermute | solution.py:397
  156.1 14.3 %collective-permute-start.8 = (bf16[1,752,256]{2,1,0:T(8,128)(2,1)S(1)}, bf16[1,752,256]{2,1,0:T(8,128)(2,1)S(1)}, u32[]{:S(2)}, u32[]{:S(2)}) collective-permute-start(bf16[1,752,256]{2,1,0:T(8,128)(2,1)S(1)} %fusion.39), channel_id=1, source_target_pairs={{8,0},{16,8},{24,16},{9,1},{17,9},{25,17},{10,2},{18,10},{26,18},{... | collective-permute-start | bytes 1155080 | tf_op jit(solution)/shard_map/ppermute | solution.py:397
  157.4 16.9 %collective-permute-start.7 = (bf16[1,752,256]{2,1,0:T(8,128)(2,1)S(1)}, bf16[1,752,256]{2,1,0:T(8,128)(2,1)S(1)}, u32[]{:S(2)}, u32[]{:S(2)}) collective-permute-start(bf16[1,752,256]{2,1,0:T(8,128)(2,1)S(1)} %fusion.38), channel_id=1, source_target_pairs={{0,8},{8,16},{16,24},{1,9},{9,17},{17,25},{2,10},{10,18},{18,26},{... | collective-permute-start | bytes 1155080 | tf_op jit(solution)/shard_map/ppermute | solution.py:397
  162.9 1.3 collective-permute-start.11
  164.3 10.0 %copy-start.3 = (bf16[2,3,720,752]{3,2,1,0:T(8,128)(2,1)S(1)}, bf16[2,3,720,752]{3,2,1,0:T(8,128)(2,1)}, u32[]{:S(2)}) copy-start(bf16[2,3,720,752]{3,2,1,0:T(8,128)(2,1)} %copy-done.2) | copy-start | bytes 19491844
  177.1 1.2 collective-permute-start.12
  177.2 1.3 collective-permute-start.13
  177.7 2.6 %copy-start.6 = (f32[9,256,256]{2,1,0:T(8,128)S(1)}, f32[9,256,256]{2,1,0:T(8,128)}, u32[]{:S(2)}) copy-start(f32[9,256,256]{2,1,0:T(8,128)} %get-tuple-element.68) | copy-start | bytes 7077892

commit v3 on v2

--- a/solution.py
+++ b/solution.py
@@ -114,7 +114,7 @@
 
 
 def middle(scale, feat, weight, target, row_weight, resp, fg, grad_w, loss, rsp, gath, acc, losses,
-           send1, recv1, out2, in2, red2, out3, in3, red3, full, sems, loss_sems):
+           send1, recv1, slopes, out2, in2, red2, out3, in3, red3, full, sems, loss_sems):
     members, lats = lax.axis_size("ens"), lax.axis_size("lat")
     me, my_lat, my_lon = lax.axis_index("ens"), lax.axis_index("lat"), lax.axis_index("lon")
     rows, taps, lon_count, channels = feat.shape
@@ -188,10 +188,21 @@
             part = lax.dot_general(feat[o, k, cols], slope, ROWDOT, preferred_element_type=jnp.float32)
             for h in range(2):
                 acc[h, pl.ds(k * channels, channels)] += part[:, h * half : (h + 1) * half]
-            fg[o, k, cols] = lax.dot_general(
-                slope, weight[k], COLDOT, preferred_element_type=jnp.float32
-            ).astype(jnp.bfloat16)
+        slopes[o, cols] = slope
         return carry + score
+
+    stages = 6
+
+    def beside(stage):
+        def spread_back(i, carry):
+            o, cols = where(i)
+            for k in range(taps):
+                fg[o, k, cols] = lax.dot_general(
+                    slopes[o, cols], weight[k], COLDOT, preferred_element_type=jnp.float32
+                ).astype(jnp.bfloat16)
+            return carry
+
+        lax.fori_loop(chunks * stage // stages, chunks * (stage + 1) // stages, spread_back, 0)
 
     score = lax.fori_loop(0, chunks, backward, jnp.zeros((8, channels), jnp.float32))
     part_loss = jnp.sum(score, axis=1, keepdims=True) * jnp.ones((8, 128), jnp.float32)
@@ -222,6 +233,7 @@
     ]
     for copy in copies:
         copy.start()
+    beside(0)
     finish(copies)
     pending += copies
     at, lat_at = at + 1, lat_at + 1
@@ -238,6 +250,7 @@
         at, lat_at = at + 1, lat_at + 1
     for copy in copies:
         copy.start()
+    beside(1)
     finish(copies)
     pending += copies
     total = red2[my_lat]
@@ -260,6 +273,7 @@
         at, lat_at = at + 1, lat_at + 1
     for copy in copies:
         copy.start()
+    beside(2)
     finish(copies)
     pending += copies
     total = red3[me]
@@ -278,6 +292,7 @@
         at += 1
     for copy in copies:
         copy.start()
+    beside(3)
     finish(copies)
     pending += copies
     mine = gathered.at[my_lon, my_lat]
@@ -287,11 +302,13 @@
         at += 1
     for copy in copies:
         copy.start()
+    beside(4)
     finish(copies)
     pending += copies
     mine = gathered.at[my_lon]
     copies = [remote(mine, mine, at, {"lon": 1 - my_lon})]
     copies[0].start()
+    beside(5)
     finish(copies)
     pending += copies
     for h in range(2):
@@ -342,6 +359,7 @@
             pltpu.VMEM((2 + lats + members, 8, 128), f32),
             pltpu.SemaphoreType.DMA((members - 1, chunks)),
             pltpu.SemaphoreType.DMA((members - 1, chunks)),
+            pltpu.VMEM((rows, lon_count, channels), bf16),
             pltpu.VMEM((lats, band, half), bf16),
             pltpu.VMEM((lats, band, half), bf16),
             pltpu.VMEM((lats, band, half), f32),

time: 186 us -> 186 us (level)
  no operation moved by 1% of the time
where the time goes in v3:
time: 186 us; the launch traced here: 182 us
  Pallas kernels  106 us (57%)
  matrix products  22.9 us (12%)
  starting transfers between devices  19.3 us (10%)
  other arithmetic  15.7 us (8%)
  waiting for transfers between devices  9.97 us (5%)
  local copies, waits for them, and re-layouts  5.71 us (3%)
  between operations  3.12 us (2%)
    pallas_call x1, Pallas kernels, run_middle(): pl.pallas_call(functools.partial(middle, scale), out_shape=[shape((rows,...  106 us
    dot_general x6, matrix products, band_row(): jnp.einsum('bjq,ebjc->eqc', band_kernels[row], feature_grad[:, row, 3 * l...  14.9 us
    ppermute x2, starting transfers between devices, lat_swap(): lax.ppermute(up, 'lat', forward)  8.78 us
    dot_general x6, matrix products, banded_row(): jnp.einsum('bjq,eqc->ebjc', kernels[row], strip, preferred_element_type=j...  6.3 us
    ppermute x2, waiting for transfers between devices, lat_swap(): lax.ppermute(down, 'lat', backward)  6.1 us
    ppermute x4, starting transfers between devices, extended_2(): lax.ppermute(lax.slice_in_dim(block, block.shape[dim] - width, None, axis...  5.5 us
    convert_element_type x1, other arithmetic, per_device(): features = jnp.where(polar_mask, rounds, banded).astype(jnp.bfloat16)  3.96 us
  transfers between devices with their start and end apart: 14, of which 5 were waited for; matrix products, arithmetic and copies ran while one was open for 11% of the time, Pallas kernels for 0%

profile of v3, /device:TPU:0, one launch (start us, length us, event | category | flops | bytes accessed | tf_op | source)
XLA Modules:
  0.0 182.4 jit_solution(6917701859881464577)
XLA Ops:
  0.6 1.9 %fusion.96 = (bf16[1,1,720,256]{3,2,1,0:T(8,128)(2,1)}, bf16[1,1,720,256]{3,2,1,0:T(8,128)(2,1)S(1)}) fusion(bf16[1,2,720,256]{3,2,1,0:T(8,128)(2,1)} %param.4), kind=kLoop, calls=%fused_computation.203 | loop fusion | bytes 1474560 | tf_op jit(solution)/shard_map/slice | solution.py:26
  2.5 4.9 %collective-permute-start = (bf16[1,1,720,256]{3,2,1,0:T(8,128)(2,1)}, bf16[1,1,720,256]{3,2,1,0:T(8,128)(2,1)S(1)}, u32[]{:S(2)}, u32[]{:S(2)}) collective-permute-start(bf16[1,1,720,256]{3,2,1,0:T(8,128)(2,1)} %get-tuple-element.20), channel_id=1, source_target_pairs={{0,8},{8,16},{16,24},{1,9},{9,17},{17,25},{2,10},{10,18},{18,26},{... | collective-permute-start | bytes 1105928 | tf_op jit(solution)/shard_map/ppermute | solution.py:25
  7.4 1.3 collective-permute-start.1
  8.7 0.7 fusion.94
  9.4 0.5 collective-permute-start.6
  9.9 0.1 fusion.58
  10.1 0.1 fusion.50
  10.2 0.1 subtract_convert_fusion.1
  10.3 0.7 convert_multiply_fusion.2
  10.9 0.2 subtract_convert_fusion
  11.2 0.1 broadcast_multiply_fusion
  11.2 3.1 %divide_convert_fusion = bf16[2,3,720,752]{3,2,1,0:T(8,128)(2,1)S(1)} fusion(f32[2]{0:T(128)S(1)} %convert_multiply_fusion.2, f32[2,3]{1,0:T(2,128)S(1)} %broadcast_multiply_fusion, f32[720,752]{1,0:T(8,128)S(1)} %subtract_convert_fusion), kind=kLoop, calls=%fused_computation.2 | loop fusion | flops 22740480 | bytes 8663072 | tf_op jit(solution)/shard_map/convert_element_type | solution.py:40
  14.3 0.0 copy-start.5
  14.4 3.5 %broadcast_select_fusion = bf16[2,3,720,752]{3,2,1,0:T(8,128)(2,1)S(1)} fusion(pred[2]{0:T(512)(128)(4,1)S(1)} %compare_or_fusion, f32[2]{0:T(128)S(1)} %convert_multiply_fusion.2, f32[2,3]{1,0:T(2,128)S(1)} %broadcast_multiply_fusion, f32[720,752]{1,0:T(8,128)S(1)} %subtract_convert_fusion), kind=kLoop, calls=%fused_computation.3 | loop fusion | flops 25989120 | bytes 8663074 | tf_op jit(solution)/shard_map/jit(_where)/select_n | solution.py:472
  17.9 0.1 constant_dynamic-update-slice_fusion.3
  18.0 1.0 fusion.13
  19.1 1.1 fusion.14
  20.1 1.1 fusion.17
  21.2 1.0 fusion.18
  22.2 3.0 %collective-permute-done.1 = bf16[1,1,720,256]{3,2,1,0:T(8,128)(2,1)S(1)} collective-permute-done((bf16[1,1,720,256]{3,2,1,0:T(8,128)(2,1)S(1)}, bf16[1,1,720,256]{3,2,1,0:T(8,128)(2,1)S(1)}, u32[]{:S(2)}, u32[]{:S(2)}) %collective-permute-start.1) | collective-permute-done | bytes 368672 | tf_op jit(solution)/shard_map/ppermute | solution.py:28
  25.2 0.8 fusion.40
  26.1 0.6 collective-permute-start.3
  26.7 0.1 collective-permute-start.4
  26.7 0.5 collective-permute-done.2
  27.3 0.1 broadcast_dynamic-update-slice_fusion.2
  27.3 0.3 multiply_dynamic-update-slice_fusion.5
  27.6 0.3 multiply_dynamic-update-slice_fusion.4
  27.9 0.1 broadcast_dynamic-update-slice_fusion.1
  28.0 0.3 multiply_dynamic-update-slice_fusion.3
  28.3 0.3 multiply_dynamic-update-slice_fusion.2
  28.6 0.1 broadcast_dynamic-update-slice_fusion
  28.7 0.3 multiply_dynamic-update-slice_fusion.1
  29.0 0.3 multiply_dynamic-update-slice_fusion
  29.3 0.1 pad_maximum_fusion
  29.3 1.1 fusion.15
  30.4 1.1 fusion.16
  31.5 4.0 %fusion.feat = bf16[2,9,720,256]{3,2,1,0:T(8,128)(2,1)} fusion(bf16[2,9,720,256]{3,2,1,0:T(8,128)(2,1)S(1)} %multiply_dynamic-update-slice_fusion, bf16[1,3,720,256]{3,2,1,0:T(8,128)(2,1)S(1)} %fusion.15, bf16[1,3,720,256]{3,2,1,0:T(8,128)(2,1)S(1)} %fusion.14, bf16[1,3,720,256]{3,2,1,0:T(8,128)(2,1)S(1)} %fusion.13, bf16[1,3,720,256]{3,2,1,0:T(8,128)(2,1)S(1)} %fusion.18, ...), kind=kLoop, calls=%fused_computation.1 | loop fusion | flops 19906560 | bytes 19906562 | tf_op jit(solution)/shard_map/convert_element_type | solution.py:458
  35.4 0.1 broadcast_in_dim.52.row_weight
  35.5 105.7 %middle.1 = (bf16[2,720,256]{2,1,0:T(8,128)(2,1)S(1)}, bf16[2,9,720,256]{3,2,1,0:T(8,128)(2,1)}, f32[9,256,256]{2,1,0:T(8,128)}, f32[8,128]{1,0:T(8,128)S(1)}) custom-call(bf16[2,9,720,256]{3,2,1,0:T(8,128)(2,1)} %fusion.feat, bf16[9,256,256]{2,1,0:T(8,128)(2,1)S(1)} %copy-done, bf16[2,720,256]{2,1,0:T(8,128)(2,1)S(1)} %copy-done.1, ...), custom_call_target="tpu_custom_call" | custom-call | tf_op jit(solution)/shard_map/middle/pallas_call | solution.py:345
  141.2 2.9 %fusion.39 = bf16[1,752,256]{2,1,0:T(8,128)(2,1)S(1)} fusion(bf16[2,3,720,752]{3,2,1,0:T(8,128)(2,1)S(1)} %broadcast_select_fusion, bf16[1,2,9,720,256]{4,3,2,1,0:T(8,128)(2,1)} %bitcast.303), kind=kOutput, calls=%fused_computation.59 | convolution fusion | flops 831844352 | bytes 4808704 | tf_op jit(solution)/shard_map/bjq,ebjc->eqc/dot_general | solution.py:492
  144.1 0.3 copy-done.4
  144.4 2.4 %fusion.28 = f32[256,752]{0,1:T(8,128)} fusion(bf16[2,3,720,752]{3,2,1,0:T(8,128)(2,1)S(1)} %broadcast_select_fusion, bf16[1,2,9,720,256]{4,3,2,1,0:T(8,128)(2,1)S(1)} %bitcast.306), kind=kOutput, calls=%fused_computation.48 | convolution fusion | flops 831651840 | bytes 5193728 | tf_op jit(solution)/shard_map/bjq,ebjc->eqc/dot_general | solution.py:492
  146.8 1.5 fusion.26
  148.3 1.5 fusion.38
  149.8 1.0 convolution_bitcast_fusion
  150.7 0.1 fusion.41
  150.9 3.4 %collective-permute-start.9 = (f32[1,3,256]{2,0,1:T(1,128)S(1)}, f32[1,3,256]{2,0,1:T(1,128)S(1)}, u32[]{:S(2)}, u32[]{:S(2)}) collective-permute-start(f32[1,3,256]{2,0,1:T(1,128)S(1)} %pad_maximum_fusion.8), channel_id=1, source_target_pairs={{0,8},{8,16},{16,24},{1,9},{9,17},{17,25},{2,10},{10,18},{18,26},{... | collective-permute-start | bytes 9224 | tf_op jit(solution)/shard_map/ppermute | solution.py:415
  154.3 1.3 collective-permute-start.10
  155.7 1.3 collective-permute-start.8
  156.9 5.4 %collective-permute-start.7 = (bf16[1,752,256]{2,1,0:T(8,128)(2,1)S(1)}, bf16[1,752,256]{2,1,0:T(8,128)(2,1)S(1)}, u32[]{:S(2)}, u32[]{:S(2)}) collective-permute-start(bf16[1,752,256]{2,1,0:T(8,128)(2,1)S(1)} %fusion.38), channel_id=1, source_target_pairs={{0,8},{8,16},{16,24},{1,9},{9,17},{17,25},{2,10},{10,18},{18,26},{... | collective-permute-start | bytes 1155080 | tf_op jit(solution)/shard_map/ppermute | solution.py:415
  162.5 0.1 collective-permute-start.11
  162.5 0.6 slice_reduce_fusion
  163.8 6.1 %collective-permute-done.8 = bf16[1,752,256]{2,1,0:T(8,128)(2,1)S(1)} collective-permute-done((bf16[1,752,256]{2,1,0:T(8,128)(2,1)S(1)}, bf16[1,752,256]{2,1,0:T(8,128)(2,1)S(1)}, u32[]{:S(2)}, u32[]{:S(2)}) %collective-permute-start.8) | collective-permute-done | bytes 385056 | tf_op jit(solution)/shard_map/ppermute | solution.py:415
  169.9 3.9 %add_bitcast_fusion = f32[1,1,752,256]{3,2,1,0:T(8,128)S(1)} fusion(bf16[1,752,256]{2,1,0:T(8,128)(2,1)S(1)} %collective-permute-done.8, f32[256,752]{0,1:T(8,128)} %fusion.28, bf16[2,3,720,752]{3,2,1,0:T(8,128)(2,1)} %copy-done.2, bf16[1,2,9,720,256]{4,3,2,1,0:T(8,128)(2,1)} %bitcast.304), kind=kOutput, calls=%fused_computation.69 | convolution fusion | flops 832229376 | bytes 6348800 | tf_op jit(solution)/shard_map/bjq,ebjc->eqc/dot_general | solution.py:492
  173.9 2.7 %add_bitcast_fusion.1 = f32[1,1,752,256]{3,2,1,0:T(8,128)S(1)} fusion(bf16[1,752,256]{2,1,0:T(8,128)(2,1)S(1)} %collective-permute-done.7, f32[256,752]{0,1:T(8,128)S(1)} %fusion.26, bf16[2,3,720,752]{3,2,1,0:T(8,128)(2,1)S(1)} %copy-done.3, bf16[1,2,9,720,256]{4,3,2,1,0:T(8,128)(2,1)} %bitcast.305), kind=kOutput, calls=%fused_computation.70 | convolution fusion | flops 832229376 | bytes 6348800 | tf_op jit(solution)/shard_map/bjq,ebjc->eqc/dot_general | solution.py:492
  176.6 0.1 collective-permute-start.12
  176.7 0.5 collective-permute-start.13
  177.2 0.3 fusion.20
  177.6 0.1 slice.656
  177.7 0.2 collective-permute-done.12
  177.9 0.2 collective-permute-done.13
  178.1 0.9 pad_maximum_fusion.1
  179.0 0.9 copy.49
  179.8 1.4 copy.50
  (63 shorter events, 0.4 us)
Async XLA Ops:
  2.5 19.7 %collective-permute-start = (bf16[1,1,720,256]{3,2,1,0:T(8,128)(2,1)}, bf16[1,1,720,256]{3,2,1,0:T(8,128)(2,1)S(1)}, u32[]{:S(2)}, u32[]{:S(2)}) collective-permute-start(bf16[1,1,720,256]{3,2,1,0:T(8,128)(2,1)} %get-tuple-element.20), channel_id=1, source_target_pairs={{0,8},{8,16},{16,24},{1,9},{9,17},{17,25},{2,10},{10,18},{18,26},{... | collective-permute-start | bytes 1105928 | tf_op jit(solution)/shard_map/ppermute | solution.py:25
  7.4 17.9 %collective-permute-start.1 = (bf16[1,1,720,256]{3,2,1,0:T(8,128)(2,1)S(1)}, bf16[1,1,720,256]{3,2,1,0:T(8,128)(2,1)S(1)}, u32[]{:S(2)}, u32[]{:S(2)}) collective-permute-start(bf16[1,1,720,256]{3,2,1,0:T(8,128)(2,1)S(1)} %get-tuple-element.21), channel_id=1, source_target_pairs={{8,0},{16,8},{24,16},{9,1},{17,9},{25,17},{10,2},{18,10},{26,18},{... | collective-permute-start | bytes 1105928 | tf_op jit(solution)/shard_map/ppermute | solution.py:28
  9.4 8.5 %collective-permute-start.5 = (bf16[1,2,16,256]{3,2,1,0:T(8,128)(2,1)S(1)}, bf16[1,2,16,256]{3,2,1,0:T(8,128)(2,1)S(1)}, u32[]{:S(2)}, u32[]{:S(2)}) collective-permute-start(bf16[1,2,16,256]{3,2,1,0:T(8,128)(2,1)S(1)} %get-tuple-element.17), channel_id=1, source_target_pairs={{0,4},{4,0},{1,5},{5,1},{2,6},{6,2},{3,7},{7,3},{8,12},{12,8},{9,1... | collective-permute-start | bytes 49160 | tf_op jit(solution)/shard_map/ppermute | solution.py:25
  9.4 8.6 %collective-permute-start.6 = (bf16[1,2,16,256]{3,2,1,0:T(8,128)(2,1)S(1)}, bf16[1,2,16,256]{3,2,1,0:T(8,128)(2,1)S(1)}, u32[]{:S(2)}, u32[]{:S(2)}) collective-permute-start(bf16[1,2,16,256]{3,2,1,0:T(8,128)(2,1)S(1)} %get-tuple-element.16), channel_id=1, source_target_pairs={{4,0},{0,4},{5,1},{1,5},{6,2},{2,6},{7,3},{3,7},{12,8},{8,12},{13,... | collective-permute-start | bytes 49160 | tf_op jit(solution)/shard_map/ppermute | solution.py:28
  14.3 3.6 %copy-start.5 = (bf16[1,2,720,256]{3,2,1,0:T(8,128)(2,1)S(1)}, bf16[1,2,720,256]{3,2,1,0:T(8,128)(2,1)}, u32[]{:S(2)}) copy-start(bf16[1,2,720,256]{3,2,1,0:T(8,128)(2,1)} %param.4) | copy-start | bytes 2211844
  17.8 130.4 %copy-start.2 = (bf16[2,3,720,752]{3,2,1,0:T(8,128)(2,1)}, bf16[2,3,720,752]{3,2,1,0:T(8,128)(2,1)S(1)}, u32[]{:S(2)}) copy-start(bf16[2,3,720,752]{3,2,1,0:T(8,128)(2,1)S(1)} %broadcast_select_fusion) | copy-start | bytes 19491844
  26.0 1.2 collective-permute-start.2
  26.1 3.2 %collective-permute-start.3 = (bf16[1,2,16,256]{3,2,1,0:T(8,128)(2,1)S(1)}, bf16[1,2,16,256]{3,2,1,0:T(8,128)(2,1)S(1)}, u32[]{:S(2)}, u32[]{:S(2)}) collective-permute-start(bf16[1,2,16,256]{3,2,1,0:T(8,128)(2,1)S(1)} %get-tuple-element.18), channel_id=1, source_target_pairs={{0,4},{4,0},{1,5},{5,1},{2,6},{6,2},{3,7},{7,3},{8,12},{12,8},{9,1... | collective-permute-start | bytes 49160 | tf_op jit(solution)/shard_map/ppermute | solution.py:25
  26.7 2.6 %collective-permute-start.4 = (bf16[1,2,16,256]{3,2,1,0:T(8,128)(2,1)S(1)}, bf16[1,2,16,256]{3,2,1,0:T(8,128)(2,1)S(1)}, u32[]{:S(2)}, u32[]{:S(2)}) collective-permute-start(bf16[1,2,16,256]{3,2,1,0:T(8,128)(2,1)S(1)} %get-tuple-element.19), channel_id=1, source_target_pairs={{4,0},{0,4},{5,1},{1,5},{6,2},{2,6},{7,3},{3,7},{12,8},{8,12},{13,... | collective-permute-start | bytes 49160 | tf_op jit(solution)/shard_map/ppermute | solution.py:28
  31.5 4.1 %copy-start = (bf16[9,256,256]{2,1,0:T(8,128)(2,1)S(1)}, bf16[9,256,256]{2,1,0:T(8,128)(2,1)}, u32[]{:S(2)}) copy-start(bf16[9,256,256]{2,1,0:T(8,128)(2,1)} %weight.1) | copy-start | bytes 3538948
  31.5 4.0 %copy-start.1 = (bf16[2,720,256]{2,1,0:T(8,128)(2,1)S(1)}, bf16[2,720,256]{2,1,0:T(8,128)(2,1)}, u32[]{:S(2)}) copy-start(bf16[2,720,256]{2,1,0:T(8,128)(2,1)} %target.1) | copy-start | bytes 2211844
  141.2 3.2 %copy-start.4 = (bf16[2,9,720,256]{3,2,1,0:T(8,128)(2,1)S(1)}, bf16[2,9,720,256]{3,2,1,0:T(8,128)(2,1)}, u32[]{:S(2)}) copy-start(bf16[2,9,720,256]{3,2,1,0:T(8,128)(2,1)} %get-tuple-element.9) | copy-start | bytes 19906564
  150.9 11.5 %collective-permute-start.9 = (f32[1,3,256]{2,0,1:T(1,128)S(1)}, f32[1,3,256]{2,0,1:T(1,128)S(1)}, u32[]{:S(2)}, u32[]{:S(2)}) collective-permute-start(f32[1,3,256]{2,0,1:T(1,128)S(1)} %pad_maximum_fusion.8), channel_id=1, source_target_pairs={{0,8},{8,16},{16,24},{1,9},{9,17},{17,25},{2,10},{10,18},{18,26},{... | collective-permute-start | bytes 9224 | tf_op jit(solution)/shard_map/ppermute | solution.py:415
  154.3 8.1 %collective-permute-start.10 = (f32[1,3,256]{2,0,1:T(1,128)S(1)}, f32[1,3,256]{2,0,1:T(1,128)S(1)}, u32[]{:S(2)}, u32[]{:S(2)}) collective-permute-start(f32[1,3,256]{2,0,1:T(1,128)S(1)} %pad_maximum_fusion.9), channel_id=1, source_target_pairs={{8,0},{16,8},{24,16},{9,1},{17,9},{25,17},{10,2},{18,10},{26,18},{... | collective-permute-start | bytes 9224 | tf_op jit(solution)/shard_map/ppermute | solution.py:415
  155.7 14.3 %collective-permute-start.8 = (bf16[1,752,256]{2,1,0:T(8,128)(2,1)S(1)}, bf16[1,752,256]{2,1,0:T(8,128)(2,1)S(1)}, u32[]{:S(2)}, u32[]{:S(2)}) collective-permute-start(bf16[1,752,256]{2,1,0:T(8,128)(2,1)S(1)} %fusion.39), channel_id=1, source_target_pairs={{8,0},{16,8},{24,16},{9,1},{17,9},{25,17},{10,2},{18,10},{26,18},{... | collective-permute-start | bytes 1155080 | tf_op jit(solution)/shard_map/ppermute | solution.py:415
  156.9 16.9 %collective-permute-start.7 = (bf16[1,752,256]{2,1,0:T(8,128)(2,1)S(1)}, bf16[1,752,256]{2,1,0:T(8,128)(2,1)S(1)}, u32[]{:S(2)}, u32[]{:S(2)}) collective-permute-start(bf16[1,752,256]{2,1,0:T(8,128)(2,1)S(1)} %fusion.38), channel_id=1, source_target_pairs={{0,8},{8,16},{16,24},{1,9},{9,17},{17,25},{2,10},{10,18},{18,26},{... | collective-permute-start | bytes 1155080 | tf_op jit(solution)/shard_map/ppermute | solution.py:415
  162.5 1.3 collective-permute-start.11
  163.8 10.0 %copy-start.3 = (bf16[2,3,720,752]{3,2,1,0:T(8,128)(2,1)S(1)}, bf16[2,3,720,752]{3,2,1,0:T(8,128)(2,1)}, u32[]{:S(2)}) copy-start(bf16[2,3,720,752]{3,2,1,0:T(8,128)(2,1)} %copy-done.2) | copy-start | bytes 19491844
  176.6 1.2 collective-permute-start.12
  176.7 1.3 collective-permute-start.13
  177.2 2.6 %copy-start.6 = (f32[9,256,256]{2,1,0:T(8,128)S(1)}, f32[9,256,256]{2,1,0:T(8,128)}, u32[]{:S(2)}) copy-start(f32[9,256,256]{2,1,0:T(8,128)} %get-tuple-element.68) | copy-start | bytes 7077892

commit v4 on v3

--- a/solution.py
+++ b/solution.py
@@ -95,7 +95,7 @@
 
 
 def pick_tile(lon_count):
-    for tile in (240, 144, 96, 80, 48, 32, 16):
+    for tile in (240, 80):
         if lon_count % tile == 0:
             return tile
     return 0
@@ -114,7 +114,7 @@
 
 
 def middle(scale, feat, weight, target, row_weight, resp, fg, grad_w, loss, rsp, gath, acc, losses,
-           send1, recv1, slopes, out2, in2, red2, out3, in3, red3, full, sems, loss_sems):
+           send1, recv1, given, send4, recv4, score_sum, slopes, out2, in2, red2, out3, in3, red3, full, sems, loss_sems):
     members, lats = lax.axis_size("ens"), lax.axis_size("lat")
     me, my_lat, my_lon = lax.axis_index("ens"), lax.axis_index("lat"), lax.axis_index("lon")
     rows, taps, lon_count, channels = feat.shape
@@ -139,12 +139,37 @@
     def where(i):
         return i // per_row, pl.ds(pl.multiple_of(lax.rem(i, per_row) * tile, 16), tile)
 
-    def gather_copy(i, p):
-        o, cols = where(i)
+    subs = 5
+    sub = tile // subs
+
+    def cell(t):
+        i = t // subs
+        first = lax.rem(i, per_row) * tile + lax.rem(t, subs) * sub
+        return i // per_row, pl.ds(pl.multiple_of(first, 16), sub), lax.rem(t, members)
+
+    def to_owner(t):
+        o, cols, owner = cell(t)
+        slot = lax.rem(owner - me + members, members) - 1
+        return pltpu.make_async_remote_copy(
+            src_ref=rsp.at[o, cols], dst_ref=gath.at[slot, o, cols],
+            send_sem=send1.at[0, t], recv_sem=recv1.at[slot, t],
+            device_id={"ens": owner}, device_id_type=MESH,
+        )
+
+    def from_member(t, p):
+        o, cols, owner = cell(t)
         return pltpu.make_async_remote_copy(
             src_ref=rsp.at[o, cols], dst_ref=gath.at[p - 1, o, cols],
-            send_sem=send1.at[p - 1, i], recv_sem=recv1.at[p - 1, i],
+            send_sem=send1.at[0, t], recv_sem=recv1.at[p - 1, t],
             device_id=peer("ens", me, members, p), device_id_type=MESH,
+        )
+
+    def to_member(t, p):
+        o, cols, owner = cell(t)
+        return pltpu.make_async_remote_copy(
+            src_ref=given.at[p - 1, o, cols], dst_ref=slopes.at[o, cols],
+            send_sem=send4.at[p - 1, t], recv_sem=recv4.at[t],
+            device_id=peer("ens", me, members, members - p), device_id_type=MESH,
         )
 
     def forward(i, carry):
@@ -153,43 +178,80 @@
         for k in range(taps):
             total = total + jnp.dot(feat[o, k, cols], weight[k], preferred_element_type=jnp.float32)
         rsp[o, cols] = total.astype(jnp.bfloat16)
-        for p in range(1, members):
-            gather_copy(i, p).start()
+        for u in range(subs):
+            t = i * subs + u
+
+            @pl.when(lax.rem(t, members) != me)
+            def _():
+                to_owner(t).start()
+
         return carry
 
     lax.fori_loop(0, chunks, forward, 0)
+    score_sum[...] = jnp.zeros_like(score_sum)
     resp[...] = rsp[...]
     acc[...] = jnp.zeros_like(acc)
 
+    def crps(t, carry):
+        o, cols, owner = cell(t)
+
+        @pl.when(owner == me)
+        def _():
+            for p in range(1, members):
+                from_member(t, p).wait_recv()
+            values = [rsp[o, cols].astype(jnp.float32)]
+            values += [gath[p - 1, o, cols].astype(jnp.float32) for p in range(1, members)]
+            truth = target[o, cols].astype(jnp.float32)
+            own_dist = jnp.zeros_like(truth)
+            pair_dist = jnp.zeros_like(truth)
+            own_slopes, pair_slopes = [], [jnp.zeros_like(truth) for _ in values]
+            for value in values:
+                miss = value - truth
+                square = miss * miss + 0.25
+                inverse = lax.rsqrt(square)
+                own_dist = own_dist + square * inverse
+                own_slopes.append(miss * inverse)
+            for m in range(members):
+                for n in range(m):
+                    gap = values[m] - values[n]
+                    square = gap * gap + 0.25
+                    inverse = lax.rsqrt(square)
+                    pair_dist = pair_dist + square * inverse
+                    tilt = gap * inverse
+                    pair_slopes[m] = pair_slopes[m] + tilt
+                    pair_slopes[n] = pair_slopes[n] - tilt
+            lat_weight = row_weight[o]
+            for p in range(members):
+                slope = lat_weight * (
+                    own_slopes[p] / members - pair_slopes[p] / (members * (members - 1))
+                )
+                if p == 0:
+                    slopes[o, cols] = slope.astype(jnp.bfloat16)
+                else:
+                    given[p - 1, o, cols] = slope.astype(jnp.bfloat16)
+                    to_member(t, p).start()
+            score = own_dist / members - pair_dist / (members * (members - 1))
+            score_sum[...] += lat_weight * jnp.sum(score.reshape(sub // 8, 8, channels), axis=0)
+
+        return carry
+
+    lax.fori_loop(0, chunks * subs, crps, 0)
+
     def backward(i, carry):
         o, cols = where(i)
-        for p in range(1, members):
-            gather_copy(i, p).wait_recv()
-        value = rsp[o, cols].astype(jnp.float32)
-        miss = value - target[o, cols].astype(jnp.float32)
-        square = miss * miss + 0.25
-        inverse = lax.rsqrt(square)
-        own_dist = square * inverse
-        own_slope = miss * inverse
-        pair_dist = jnp.zeros_like(value)
-        pair_slope = jnp.zeros_like(value)
-        for p in range(1, members):
-            gap = value - gath[p - 1, o, cols].astype(jnp.float32)
-            square = gap * gap + 0.25
-            inverse = lax.rsqrt(square)
-            pair_dist = pair_dist + square * inverse
-            pair_slope = pair_slope + gap * inverse
-        lat_weight = row_weight[o]
-        score = own_dist / members - pair_dist / (2 * members * (members - 1))
-        slope = lat_weight * (own_slope / members - pair_slope / (members * (members - 1)))
-        slope = slope.astype(jnp.bfloat16)
-        score = lat_weight * jnp.sum(score.reshape(tile // 8, 8, channels), axis=0)
+        for u in range(subs):
+            t = i * subs + u
+
+            @pl.when(lax.rem(t, members) != me)
+            def _():
+                to_member(t, 1).wait_recv()
+
+        slope = slopes[o, cols]
         for k in range(taps):
             part = lax.dot_general(feat[o, k, cols], slope, ROWDOT, preferred_element_type=jnp.float32)
             for h in range(2):
                 acc[h, pl.ds(k * channels, channels)] += part[:, h * half : (h + 1) * half]
-        slopes[o, cols] = slope
-        return carry + score
+        return carry
 
     stages = 6
 
@@ -204,7 +266,8 @@
 
         lax.fori_loop(chunks * stage // stages, chunks * (stage + 1) // stages, spread_back, 0)
 
-    score = lax.fori_loop(0, chunks, backward, jnp.zeros((8, channels), jnp.float32))
+    lax.fori_loop(0, chunks, backward, 0)
+    score = score_sum[...]
     part_loss = jnp.sum(score, axis=1, keepdims=True) * jnp.ones((8, 128), jnp.float32)
 
     def remote(src, dst, at, other):
@@ -318,12 +381,19 @@
     for copy in pending:
         copy.wait_send()
 
-    def drain(i, carry):
-        for p in range(1, members):
-            gather_copy(i, p).wait_send()
+    def drain(t, carry):
+        @pl.when(lax.rem(t, members) != me)
+        def _():
+            to_owner(t).wait_send()
+
+        @pl.when(lax.rem(t, members) == me)
+        def _():
+            for p in range(1, members):
+                to_member(t, p).wait_send()
+
         return carry
 
-    lax.fori_loop(0, chunks, drain, 0)
+    lax.fori_loop(0, chunks * subs, drain, 0)
 
 
 def full_split(full, members):
@@ -357,8 +427,12 @@
             pltpu.VMEM((members - 1, rows, lon_count, channels), bf16),
             pltpu.VMEM((2, flat, half), f32),
             pltpu.VMEM((2 + lats + members, 8, 128), f32),
-            pltpu.SemaphoreType.DMA((members - 1, chunks)),
-            pltpu.SemaphoreType.DMA((members - 1, chunks)),
+            pltpu.SemaphoreType.DMA((1, 5 * chunks)),
+            pltpu.SemaphoreType.DMA((members - 1, 5 * chunks)),
+            pltpu.VMEM((members - 1, rows, lon_count, channels), bf16),
+            pltpu.SemaphoreType.DMA((members - 1, 5 * chunks)),
+            pltpu.SemaphoreType.DMA((5 * chunks,)),
+            pltpu.VMEM((8, channels), f32),
             pltpu.VMEM((rows, lon_count, channels), bf16),
             pltpu.VMEM((lats, band, half), bf16),
             pltpu.VMEM((lats, band, half), bf16),

time: 186 us -> 155 us (0.83)
  the two profiles are of different devices: /device:TPU:0 before, /device:TPU:7 now
where the time goes in v4:
time: 155 us
  Pallas kernels  77.3 us (50%)
  matrix products  22.9 us (15%)
  starting transfers between devices  19.8 us (13%)
  other arithmetic  15.7 us (10%)
  waiting for transfers between devices  10.4 us (7%)
  local copies, waits for them, and re-layouts  5.71 us (4%)
  between operations  3.11 us (2%)
    pallas_call x1, Pallas kernels, run_middle(): pl.pallas_call(functools.partial(middle, scale), out_shape=[shape((rows,...  77.3 us
    dot_general x6, matrix products, band_row(): jnp.einsum('bjq,ebjc->eqc', band_kernels[row], feature_grad[:, row, 3 * l...  14.9 us
    ppermute x2, starting transfers between devices, lat_swap(): lax.ppermute(down, 'lat', backward)  7.34 us
    dot_general x6, matrix products, banded_row(): jnp.einsum('bjq,eqc->ebjc', kernels[row], strip, preferred_element_type=j...  6.3 us
    ppermute x2, waiting for transfers between devices, lat_swap(): lax.ppermute(up, 'lat', forward)  5.45 us
    ppermute x4, starting transfers between devices, extended_2(): lax.ppermute(lax.slice_in_dim(block, 0, width, axis=dim), axis, backward)  4.59 us
    ppermute x2, waiting for transfers between devices, lat_swap(): lax.ppermute(down, 'lat', backward)  4.12 us
    convert_element_type x1, other arithmetic, per_device(): features = jnp.where(polar_mask, rounds, banded).astype(jnp.bfloat16)  3.96 us
  transfers between devices with their start and end apart: 14, of which 5 were waited for; matrix products, arithmetic and copies ran while one was open for 13% of the time, Pallas kernels for 0%

profile of v4, /device:TPU:7, one launch (start us, length us, event | category | flops | bytes accessed | tf_op | source)
XLA Modules:
  0.0 154.9 jit_solution(12635747229570468781)
XLA Ops:
  0.6 1.9 %fusion.96 = (bf16[1,1,720,256]{3,2,1,0:T(8,128)(2,1)}, bf16[1,1,720,256]{3,2,1,0:T(8,128)(2,1)S(1)}) fusion(bf16[1,2,720,256]{3,2,1,0:T(8,128)(2,1)} %param.4), kind=kLoop, calls=%fused_computation.203 | loop fusion | bytes 1474560 | tf_op jit(solution)/shard_map/slice | solution.py:26
  2.5 1.3 collective-permute-start
  3.8 4.0 %collective-permute-start.1 = (bf16[1,1,720,256]{3,2,1,0:T(8,128)(2,1)S(1)}, bf16[1,1,720,256]{3,2,1,0:T(8,128)(2,1)S(1)}, u32[]{:S(2)}, u32[]{:S(2)}) collective-permute-start(bf16[1,1,720,256]{3,2,1,0:T(8,128)(2,1)S(1)} %get-tuple-element.21), channel_id=1, source_target_pairs={{8,0},{16,8},{24,16},{9,1},{17,9},{25,17},{10,2},{18,10},{26,18},{... | collective-permute-start | bytes 1105928 | tf_op jit(solution)/shard_map/ppermute | solution.py:28
  7.8 0.7 fusion.94
  8.6 1.2 collective-permute-start.5
  9.8 0.1 fusion.58
  10.0 0.1 fusion.50
  10.1 0.1 subtract_convert_fusion.1
  10.1 0.7 convert_multiply_fusion.2
  10.8 0.2 subtract_convert_fusion
  11.0 0.1 broadcast_multiply_fusion
  11.1 3.1 %divide_convert_fusion = bf16[2,3,720,752]{3,2,1,0:T(8,128)(2,1)S(1)} fusion(f32[2]{0:T(128)S(1)} %convert_multiply_fusion.2, f32[2,3]{1,0:T(2,128)S(1)} %broadcast_multiply_fusion, f32[720,752]{1,0:T(8,128)S(1)} %subtract_convert_fusion), kind=kLoop, calls=%fused_computation.2 | loop fusion | flops 22740480 | bytes 8663072 | tf_op jit(solution)/shard_map/convert_element_type | solution.py:40
  14.2 3.5 %broadcast_select_fusion = bf16[2,3,720,752]{3,2,1,0:T(8,128)(2,1)S(1)} fusion(pred[2]{0:T(512)(128)(4,1)S(1)} %compare_or_fusion, f32[2]{0:T(128)S(1)} %convert_multiply_fusion.2, f32[2,3]{1,0:T(2,128)S(1)} %broadcast_multiply_fusion, f32[720,752]{1,0:T(8,128)S(1)} %subtract_convert_fusion), kind=kLoop, calls=%fused_computation.3 | loop fusion | flops 25989120 | bytes 8663074 | tf_op jit(solution)/shard_map/jit(_where)/select_n | solution.py:546
  17.8 0.1 constant_dynamic-update-slice_fusion.3
  17.9 1.0 fusion.13
  18.9 1.1 fusion.14
  20.0 1.1 fusion.17
  21.1 1.0 fusion.18
  22.1 0.8 fusion.40
  22.9 0.5 collective-permute-start.2
  23.5 0.1 collective-permute-start.3
  23.6 0.5 collective-permute-start.4
  24.1 0.2 collective-permute-done.2
  24.3 0.1 broadcast_dynamic-update-slice_fusion.2
  24.4 0.3 multiply_dynamic-update-slice_fusion.5
  24.7 0.3 multiply_dynamic-update-slice_fusion.4
  25.0 0.1 broadcast_dynamic-update-slice_fusion.1
  25.1 0.3 multiply_dynamic-update-slice_fusion.3
  25.4 0.3 multiply_dynamic-update-slice_fusion.2
  25.7 0.1 broadcast_dynamic-update-slice_fusion
  25.7 0.3 multiply_dynamic-update-slice_fusion.1
  26.0 0.3 multiply_dynamic-update-slice_fusion
  26.3 0.1 pad_maximum_fusion
  26.4 1.1 fusion.15
  27.5 1.0 fusion.16
  28.5 4.0 %fusion.feat = bf16[2,9,720,256]{3,2,1,0:T(8,128)(2,1)} fusion(bf16[2,9,720,256]{3,2,1,0:T(8,128)(2,1)S(1)} %multiply_dynamic-update-slice_fusion, bf16[1,3,720,256]{3,2,1,0:T(8,128)(2,1)S(1)} %fusion.15, bf16[1,3,720,256]{3,2,1,0:T(8,128)(2,1)S(1)} %fusion.14, bf16[1,3,720,256]{3,2,1,0:T(8,128)(2,1)S(1)} %fusion.13, bf16[1,3,720,256]{3,2,1,0:T(8,128)(2,1)S(1)} %fusion.18, ...), kind=kLoop, calls=%fused_computation.1 | loop fusion | flops 19906560 | bytes 19906562 | tf_op jit(solution)/shard_map/convert_element_type | solution.py:532
  32.5 0.1 broadcast_in_dim.52.row_weight
  32.6 77.3 %middle.1 = (bf16[2,720,256]{2,1,0:T(8,128)(2,1)S(1)}, bf16[2,9,720,256]{3,2,1,0:T(8,128)(2,1)}, f32[9,256,256]{2,1,0:T(8,128)}, f32[8,128]{1,0:T(8,128)S(1)}) custom-call(bf16[2,9,720,256]{3,2,1,0:T(8,128)(2,1)} %fusion.feat, bf16[9,256,256]{2,1,0:T(8,128)(2,1)S(1)} %copy-done, bf16[2,720,256]{2,1,0:T(8,128)(2,1)S(1)} %copy-done.1, ...), custom_call_target="tpu_custom_call" | custom-call | tf_op jit(solution)/shard_map/middle/pallas_call | solution.py:415
  109.9 2.9 %fusion.39 = bf16[1,752,256]{2,1,0:T(8,128)(2,1)S(1)} fusion(bf16[2,3,720,752]{3,2,1,0:T(8,128)(2,1)S(1)} %broadcast_select_fusion, bf16[1,2,9,720,256]{4,3,2,1,0:T(8,128)(2,1)} %bitcast.303), kind=kOutput, calls=%fused_computation.59 | convolution fusion | flops 831844352 | bytes 4808704 | tf_op jit(solution)/shard_map/bjq,ebjc->eqc/dot_general | solution.py:566
  112.8 0.3 copy-done.4
  113.1 2.4 %fusion.28 = f32[256,752]{0,1:T(8,128)} fusion(bf16[2,3,720,752]{3,2,1,0:T(8,128)(2,1)S(1)} %broadcast_select_fusion, bf16[1,2,9,720,256]{4,3,2,1,0:T(8,128)(2,1)S(1)} %bitcast.306), kind=kOutput, calls=%fused_computation.48 | convolution fusion | flops 831651840 | bytes 5193728 | tf_op jit(solution)/shard_map/bjq,ebjc->eqc/dot_general | solution.py:566
  115.5 1.5 fusion.26
  117.0 1.5 fusion.38
  118.5 1.0 convolution_bitcast_fusion
  119.4 0.1 fusion.41
  119.6 1.3 collective-permute-start.9
  120.9 4.0 %collective-permute-start.10 = (f32[1,3,256]{2,0,1:T(1,128)S(1)}, f32[1,3,256]{2,0,1:T(1,128)S(1)}, u32[]{:S(2)}, u32[]{:S(2)}) collective-permute-start(f32[1,3,256]{2,0,1:T(1,128)S(1)} %pad_maximum_fusion.9), channel_id=1, source_target_pairs={{8,0},{16,8},{24,16},{9,1},{17,9},{25,17},{10,2},{18,10},{26,18},{... | collective-permute-start | bytes 9224 | tf_op jit(solution)/shard_map/ppermute | solution.py:489
  125.0 3.3 %collective-permute-start.8 = (bf16[1,752,256]{2,1,0:T(8,128)(2,1)S(1)}, bf16[1,752,256]{2,1,0:T(8,128)(2,1)S(1)}, u32[]{:S(2)}, u32[]{:S(2)}) collective-permute-start(bf16[1,752,256]{2,1,0:T(8,128)(2,1)S(1)} %fusion.39), channel_id=1, source_target_pairs={{8,0},{16,8},{24,16},{9,1},{17,9},{25,17},{10,2},{18,10},{26,18},{... | collective-permute-start | bytes 1155080 | tf_op jit(solution)/shard_map/ppermute | solution.py:489
  128.3 1.3 collective-permute-start.7
  129.7 0.8 collective-permute-start.11
  130.5 0.6 slice_reduce_fusion
  131.8 4.1 %collective-permute-done.8 = bf16[1,752,256]{2,1,0:T(8,128)(2,1)S(1)} collective-permute-done((bf16[1,752,256]{2,1,0:T(8,128)(2,1)S(1)}, bf16[1,752,256]{2,1,0:T(8,128)(2,1)S(1)}, u32[]{:S(2)}, u32[]{:S(2)}) %collective-permute-start.8) | collective-permute-done | bytes 385056 | tf_op jit(solution)/shard_map/ppermute | solution.py:489
  135.9 3.9 %add_bitcast_fusion = f32[1,1,752,256]{3,2,1,0:T(8,128)S(1)} fusion(bf16[1,752,256]{2,1,0:T(8,128)(2,1)S(1)} %collective-permute-done.8, f32[256,752]{0,1:T(8,128)} %fusion.28, bf16[2,3,720,752]{3,2,1,0:T(8,128)(2,1)} %copy-done.2, bf16[1,2,9,720,256]{4,3,2,1,0:T(8,128)(2,1)} %bitcast.304), kind=kOutput, calls=%fused_computation.69 | convolution fusion | flops 832229376 | bytes 6348800 | tf_op jit(solution)/shard_map/bjq,ebjc->eqc/dot_general | solution.py:566
  139.8 5.4 %collective-permute-done.7 = bf16[1,752,256]{2,1,0:T(8,128)(2,1)S(1)} collective-permute-done((bf16[1,752,256]{2,1,0:T(8,128)(2,1)S(1)}, bf16[1,752,256]{2,1,0:T(8,128)(2,1)S(1)}, u32[]{:S(2)}, u32[]{:S(2)}) %collective-permute-start.7) | collective-permute-done | bytes 385056 | tf_op jit(solution)/shard_map/ppermute | solution.py:489
  145.3 2.7 %add_bitcast_fusion.1 = f32[1,1,752,256]{3,2,1,0:T(8,128)S(1)} fusion(bf16[1,752,256]{2,1,0:T(8,128)(2,1)S(1)} %collective-permute-done.7, f32[256,752]{0,1:T(8,128)S(1)} %fusion.26, bf16[2,3,720,752]{3,2,1,0:T(8,128)(2,1)S(1)} %copy-done.3, bf16[1,2,9,720,256]{4,3,2,1,0:T(8,128)(2,1)} %bitcast.305), kind=kOutput, calls=%fused_computation.70 | convolution fusion | flops 832229376 | bytes 6348800 | tf_op jit(solution)/shard_map/bjq,ebjc->eqc/dot_general | solution.py:566
  148.1 1.4 collective-permute-start.12
  149.4 0.1 collective-permute-start.13
  149.5 0.3 fusion.20
  149.9 0.1 slice.656
  149.9 0.3 collective-permute-done.12
  150.3 0.3 collective-permute-done.13
  150.6 0.9 pad_maximum_fusion.1
  151.5 0.9 copy.49
  152.4 1.4 copy.50
  (63 shorter events, 0.4 us)
Async XLA Ops:
  2.5 19.6 %collective-permute-start = (bf16[1,1,720,256]{3,2,1,0:T(8,128)(2,1)}, bf16[1,1,720,256]{3,2,1,0:T(8,128)(2,1)S(1)}, u32[]{:S(2)}, u32[]{:S(2)}) collective-permute-start(bf16[1,1,720,256]{3,2,1,0:T(8,128)(2,1)} %get-tuple-element.20), channel_id=1, source_target_pairs={{0,8},{8,16},{16,24},{1,9},{9,17},{17,25},{2,10},{10,18},{18,26},{... | collective-permute-start | bytes 1105928 | tf_op jit(solution)/shard_map/ppermute | solution.py:25
  3.8 18.3 %collective-permute-start.1 = (bf16[1,1,720,256]{3,2,1,0:T(8,128)(2,1)S(1)}, bf16[1,1,720,256]{3,2,1,0:T(8,128)(2,1)S(1)}, u32[]{:S(2)}, u32[]{:S(2)}) collective-permute-start(bf16[1,1,720,256]{3,2,1,0:T(8,128)(2,1)S(1)} %get-tuple-element.21), channel_id=1, source_target_pairs={{8,0},{16,8},{24,16},{9,1},{17,9},{25,17},{10,2},{18,10},{26,18},{... | collective-permute-start | bytes 1105928 | tf_op jit(solution)/shard_map/ppermute | solution.py:28
  8.6 9.2 %collective-permute-start.5 = (bf16[1,2,16,256]{3,2,1,0:T(8,128)(2,1)S(1)}, bf16[1,2,16,256]{3,2,1,0:T(8,128)(2,1)S(1)}, u32[]{:S(2)}, u32[]{:S(2)}) collective-permute-start(bf16[1,2,16,256]{3,2,1,0:T(8,128)(2,1)S(1)} %get-tuple-element.17), channel_id=1, source_target_pairs={{0,4},{4,0},{1,5},{5,1},{2,6},{6,2},{3,7},{7,3},{8,12},{12,8},{9,1... | collective-permute-start | bytes 49160 | tf_op jit(solution)/shard_map/ppermute | solution.py:25
  9.8 8.1 %collective-permute-start.6 = (bf16[1,2,16,256]{3,2,1,0:T(8,128)(2,1)S(1)}, bf16[1,2,16,256]{3,2,1,0:T(8,128)(2,1)S(1)}, u32[]{:S(2)}, u32[]{:S(2)}) collective-permute-start(bf16[1,2,16,256]{3,2,1,0:T(8,128)(2,1)S(1)} %get-tuple-element.16), channel_id=1, source_target_pairs={{4,0},{0,4},{5,1},{1,5},{6,2},{2,6},{7,3},{3,7},{12,8},{8,12},{13,... | collective-permute-start | bytes 49160 | tf_op jit(solution)/shard_map/ppermute | solution.py:28
  14.2 3.6 %copy-start.5 = (bf16[1,2,720,256]{3,2,1,0:T(8,128)(2,1)S(1)}, bf16[1,2,720,256]{3,2,1,0:T(8,128)(2,1)}, u32[]{:S(2)}) copy-start(bf16[1,2,720,256]{3,2,1,0:T(8,128)(2,1)} %param.4) | copy-start | bytes 2211844
  17.7 99.2 %copy-start.2 = (bf16[2,3,720,752]{3,2,1,0:T(8,128)(2,1)}, bf16[2,3,720,752]{3,2,1,0:T(8,128)(2,1)S(1)}, u32[]{:S(2)}) copy-start(bf16[2,3,720,752]{3,2,1,0:T(8,128)(2,1)S(1)} %broadcast_select_fusion) | copy-start | bytes 19491844
  22.9 1.4 collective-permute-start.2
  23.5 2.8 %collective-permute-start.3 = (bf16[1,2,16,256]{3,2,1,0:T(8,128)(2,1)S(1)}, bf16[1,2,16,256]{3,2,1,0:T(8,128)(2,1)S(1)}, u32[]{:S(2)}, u32[]{:S(2)}) collective-permute-start(bf16[1,2,16,256]{3,2,1,0:T(8,128)(2,1)S(1)} %get-tuple-element.18), channel_id=1, source_target_pairs={{0,4},{4,0},{1,5},{5,1},{2,6},{6,2},{3,7},{7,3},{8,12},{12,8},{9,1... | collective-permute-start | bytes 49160 | tf_op jit(solution)/shard_map/ppermute | solution.py:25
  23.6 2.8 %collective-permute-start.4 = (bf16[1,2,16,256]{3,2,1,0:T(8,128)(2,1)S(1)}, bf16[1,2,16,256]{3,2,1,0:T(8,128)(2,1)S(1)}, u32[]{:S(2)}, u32[]{:S(2)}) collective-permute-start(bf16[1,2,16,256]{3,2,1,0:T(8,128)(2,1)S(1)} %get-tuple-element.19), channel_id=1, source_target_pairs={{4,0},{0,4},{5,1},{1,5},{6,2},{2,6},{7,3},{3,7},{12,8},{8,12},{13,... | collective-permute-start | bytes 49160 | tf_op jit(solution)/shard_map/ppermute | solution.py:28
  28.5 4.1 %copy-start = (bf16[9,256,256]{2,1,0:T(8,128)(2,1)S(1)}, bf16[9,256,256]{2,1,0:T(8,128)(2,1)}, u32[]{:S(2)}) copy-start(bf16[9,256,256]{2,1,0:T(8,128)(2,1)} %weight.1) | copy-start | bytes 3538948
  28.5 4.0 %copy-start.1 = (bf16[2,720,256]{2,1,0:T(8,128)(2,1)S(1)}, bf16[2,720,256]{2,1,0:T(8,128)(2,1)}, u32[]{:S(2)}) copy-start(bf16[2,720,256]{2,1,0:T(8,128)(2,1)} %target.1) | copy-start | bytes 2211844
  109.9 3.2 %copy-start.4 = (bf16[2,9,720,256]{3,2,1,0:T(8,128)(2,1)S(1)}, bf16[2,9,720,256]{3,2,1,0:T(8,128)(2,1)}, u32[]{:S(2)}) copy-start(bf16[2,9,720,256]{3,2,1,0:T(8,128)(2,1)} %get-tuple-element.9) | copy-start | bytes 19906564
  119.6 10.1 %collective-permute-start.9 = (f32[1,3,256]{2,0,1:T(1,128)S(1)}, f32[1,3,256]{2,0,1:T(1,128)S(1)}, u32[]{:S(2)}, u32[]{:S(2)}) collective-permute-start(f32[1,3,256]{2,0,1:T(1,128)S(1)} %pad_maximum_fusion.8), channel_id=1, source_target_pairs={{0,8},{8,16},{16,24},{1,9},{9,17},{17,25},{2,10},{10,18},{18,26},{... | collective-permute-start | bytes 9224 | tf_op jit(solution)/shard_map/ppermute | solution.py:489
  120.9 8.7 %collective-permute-start.10 = (f32[1,3,256]{2,0,1:T(1,128)S(1)}, f32[1,3,256]{2,0,1:T(1,128)S(1)}, u32[]{:S(2)}, u32[]{:S(2)}) collective-permute-start(f32[1,3,256]{2,0,1:T(1,128)S(1)} %pad_maximum_fusion.9), channel_id=1, source_target_pairs={{8,0},{16,8},{24,16},{9,1},{17,9},{25,17},{10,2},{18,10},{26,18},{... | collective-permute-start | bytes 9224 | tf_op jit(solution)/shard_map/ppermute | solution.py:489
  125.0 11.0 %collective-permute-start.8 = (bf16[1,752,256]{2,1,0:T(8,128)(2,1)S(1)}, bf16[1,752,256]{2,1,0:T(8,128)(2,1)S(1)}, u32[]{:S(2)}, u32[]{:S(2)}) collective-permute-start(bf16[1,752,256]{2,1,0:T(8,128)(2,1)S(1)} %fusion.39), channel_id=1, source_target_pairs={{8,0},{16,8},{24,16},{9,1},{17,9},{25,17},{10,2},{18,10},{26,18},{... | collective-permute-start | bytes 1155080 | tf_op jit(solution)/shard_map/ppermute | solution.py:489
  128.3 17.0 %collective-permute-start.7 = (bf16[1,752,256]{2,1,0:T(8,128)(2,1)S(1)}, bf16[1,752,256]{2,1,0:T(8,128)(2,1)S(1)}, u32[]{:S(2)}, u32[]{:S(2)}) collective-permute-start(bf16[1,752,256]{2,1,0:T(8,128)(2,1)S(1)} %fusion.38), channel_id=1, source_target_pairs={{0,8},{8,16},{16,24},{1,9},{9,17},{17,25},{2,10},{10,18},{18,26},{... | collective-permute-start | bytes 1155080 | tf_op jit(solution)/shard_map/ppermute | solution.py:489
  129.7 2.1 %collective-permute-start.11 = (f32[1,3,2,256]{3,2,1,0:T(2,128)S(1)}, f32[1,3,2,256]{3,2,1,0:T(2,128)S(1)}, u32[]{:S(2)}, u32[]{:S(2)}) collective-permute-start(f32[1,3,2,256]{3,2,1,0:T(2,128)S(1)} %pad_maximum_fusion.7), channel_id=1, source_target_pairs={{0,4},{4,0},{1,5},{5,1},{2,6},{6,2},{3,7},{7,3},{8,12},{12,8},{9,1... | collective-permute-start | bytes 18440 | tf_op jit(solution)/shard_map/ppermute | solution.py:481
  131.8 13.5 %copy-start.3 = (bf16[2,3,720,752]{3,2,1,0:T(8,128)(2,1)S(1)}, bf16[2,3,720,752]{3,2,1,0:T(8,128)(2,1)}, u32[]{:S(2)}) copy-start(bf16[2,3,720,752]{3,2,1,0:T(8,128)(2,1)} %copy-done.2) | copy-start | bytes 19491844
  148.1 2.2 %collective-permute-start.12 = (bf16[1,2,16,256]{3,2,1,0:T(8,128)(2,1)S(1)}, bf16[1,2,16,256]{3,2,1,0:T(8,128)(2,1)S(1)}, u32[]{:S(2)}, u32[]{:S(2)}) collective-permute-start(bf16[1,2,16,256]{3,2,1,0:T(8,128)(2,1)S(1)} %get-tuple-element.14), channel_id=1, source_target_pairs={{0,4},{4,0},{1,5},{5,1},{2,6},{6,2},{3,7},{7,3},{8,12},{12,8},{9,1... | collective-permute-start | bytes 49160 | tf_op jit(solution)/shard_map/ppermute | solution.py:25
  149.4 1.2 collective-permute-start.13
  149.5 2.9 %copy-start.6 = (f32[9,256,256]{2,1,0:T(8,128)S(1)}, f32[9,256,256]{2,1,0:T(8,128)}, u32[]{:S(2)}) copy-start(f32[9,256,256]{2,1,0:T(8,128)} %get-tuple-element.68) | copy-start | bytes 7077892
